TPU v7x, 32 devices: a whole 2x2x4 slice. The times are simulated.
32 devices in a mesh: dop: 4 (over y, core), rng: 8 (over z, x).
Axes of the slice: x: 2, y: 2, z: 4, core: 2. Of those that a mesh axis runs over, the one named last changes fastest.
Arguments:
- echoes: bfloat16 [2048, 2, 32, 128], P(('rng', 'dop')), may hold values from -60 to 60
- training: int32 [128, 2048], P('dop', 'rng'), may hold values 0 or 1
- look_index: int32 [64], replicated, may hold values from 0 to 255
Outputs:
- beam_output: float32 [128, 2, 64, 2048], P('dop', None, None, 'rng')
All inputs are finite; a program needn't handle non-finite values. No bound on the sum of `training` on one device may be relied on, other than what follows from the above.
Results may differ from a plain program's by a relative error of at most 0.012.
The roundings to bfloat16 on the way count: a program that leaves them out, or rounds other values in their place, can miss the bound.
Values may be sent and summed in bfloat16 or wider, within the bound.
A program may use at most 128 MiB of HBM per device.

v0:
```python
import jax
import jax.numpy as jnp
from jax import lax
from jax.sharding import PartitionSpec as P

CH = 32
PULSES = 128
LOOKS = 64
ANGLES = 256
SNAP = 192


loading = 0.1
epsilon = 1e-06
block_pairs = ((0, 0), (0, 1), (0, 2), (1, 1), (1, 2), (2, 2))


def padded(block, sides, width):
    for axis, dim in sides:
        count = lax.axis_size(axis)
        forward = [(i, i + 1) for i in range(count - 1)]
        forward.append((count - 1, 0))
        backward = [(target, source) for source, target in forward]
        low = lax.ppermute(
            lax.slice_in_dim(block, block.shape[dim] - width, None, axis=dim), axis, forward
        )
        high = lax.ppermute(lax.slice_in_dim(block, 0, width, axis=dim), axis, backward)
        block = jnp.concatenate([low, block, high], axis=dim)
    return block


def twiddles():
    pulse_ids = jnp.arange(PULSES, dtype=jnp.int32)
    phase_ids = pulse_ids[:, None] * pulse_ids[None, :] % PULSES
    angles = phase_ids.astype(jnp.float32) * (2.0 * jnp.pi / PULSES)
    return jnp.concatenate([jnp.cos(angles), jnp.sin(angles)], axis=0).astype(jnp.bfloat16)


def doppler_spectra(echo_rows, twiddle):
    product = jnp.einsum("kp,rqcp->krqc", twiddle, echo_rows, preferred_element_type=jnp.float32)
    cosine = product[:PULSES]
    sine = product[PULSES:]
    real_part = cosine[:, :, 0] + sine[:, :, 1]
    imag_part = cosine[:, :, 1] - sine[:, :, 0]
    return (
        jnp.stack([real_part, imag_part], axis=2)
        .reshape(PULSES, echo_rows.shape[0], 2 * CH)
        .astype(jnp.bfloat16)
    )


def steering(look_index):
    sines = -1.0 + (2.0 * look_index.astype(jnp.float32) + 1.0) / ANGLES
    channel_ids = jnp.arange(CH).astype(jnp.float32)
    phases = jnp.pi * channel_ids[:, None] * sines[None, :]
    zeros = jnp.zeros((CH, LOOKS), jnp.float32)
    return jnp.stack([zeros, zeros, jnp.cos(phases), jnp.sin(phases), zeros, zeros]).reshape(
        SNAP, LOOKS
    )


def mvdr_weights(upper_blocks, steer):
    bin_count = upper_blocks.shape[0]
    gram_grid = upper_blocks.reshape(bin_count, 6, CH, 2, CH)
    lower_rows = jnp.stack([-gram_grid[:, :, :, 1], gram_grid[:, :, :, 0]], axis=3)
    blocks = jnp.stack([gram_grid, lower_rows], axis=2).reshape(bin_count, 6, 2 * CH, 2 * CH)
    row_list = []
    for left_pos in range(3):
        pieces = []
        for right_pos in range(3):
            if left_pos <= right_pos:
                pieces.append(blocks[:, block_pairs.index((left_pos, right_pos))])
            else:
                pieces.append(
                    jnp.swapaxes(blocks[:, block_pairs.index((right_pos, left_pos))], 1, 2)
                )
        row_list.append(jnp.concatenate(pieces, axis=2))
    matrix = jnp.concatenate(row_list, axis=1)
    power = jnp.trace(matrix, axis1=1, axis2=2) / SNAP + epsilon
    regular = matrix / power[:, None, None] + loading * jnp.eye(SNAP, dtype=jnp.float32)
    factor = jnp.linalg.cholesky(regular)
    targets = jnp.broadcast_to(steer, (bin_count, SNAP, LOOKS))
    forward = lax.linalg.triangular_solve(factor, targets, left_side=True, lower=True)
    solved = lax.linalg.triangular_solve(
        factor, forward, left_side=True, lower=True, transpose_a=True
    )
    gains = jnp.sum(targets * solved, axis=1)
    unit = solved / jnp.sqrt(gains)[:, None, :]
    shaped = unit.reshape(bin_count, 3, 2, CH, LOOKS)
    rotated = jnp.stack([-shaped[:, :, 1], shaped[:, :, 0]], axis=2)
    return jnp.concatenate([unit, rotated.reshape(bin_count, SNAP, LOOKS)], axis=2).astype(
        jnp.bfloat16
    )


def body(echoes, training, look_index):
    spectra = doppler_spectra(echoes, twiddles())
    groups = lax.axis_size("dop")
    bins_here = PULSES // groups
    turned = lax.all_to_all(spectra, "dop", split_axis=0, concat_axis=1, tiled=True)
    edged = padded(turned, (("dop", 0),), 1)
    mask_rows = training.astype(jnp.bfloat16)
    steer = steering(look_index)
    share_bins = bins_here // lax.axis_size("rng")
    bin_count = share_bins * lax.axis_size("rng")
    slab_rows = edged
    weighting = mask_rows[:, :, None]
    products = []
    for left_pos, right_pos in block_pairs:
        masked = slab_rows[left_pos : left_pos + bin_count] * weighting
        products.append(
            jnp.einsum(
                "krn,krm->knm",
                masked,
                slab_rows[right_pos : right_pos + bin_count],
                preferred_element_type=jnp.float32,
            )
        )
    gram_blocks = jnp.stack(products, axis=1).reshape(bin_count, 6, 2, CH, 2, CH)
    flip_sign = jnp.array([1.0, -1.0], jnp.float32).reshape(1, 1, 1, 2, 1)
    upper_half = gram_blocks[:, :, 0] + flip_sign * gram_blocks[:, :, 1][:, :, :, ::-1, :]
    my_gram = lax.psum_scatter(
        upper_half.reshape(bin_count, 6 * CH, 2 * CH), "rng", scatter_dimension=0, tiled=True
    )
    weight_piece = lax.all_gather(mvdr_weights(my_gram, steer), "rng", axis=0, tiled=True)
    bin_count = weight_piece.shape[0]
    slab_rows = edged
    weight_parts = weight_piece.reshape(bin_count, 3, 2 * CH, 2 * LOOKS)
    summed = jnp.einsum(
        "knj,krn->kjr",
        weight_parts[:, 0],
        slab_rows[0:bin_count],
        preferred_element_type=jnp.float32,
    )
    for position in range(1, 3):
        summed = summed + jnp.einsum(
            "knj,krn->kjr",
            weight_parts[:, position],
            slab_rows[position : position + bin_count],
            preferred_element_type=jnp.float32,
        )
    return summed.reshape(bin_count, 2, LOOKS, slab_rows.shape[1])


def solution(mesh):
    in_specs = (P(("rng", "dop"), None, None, None), P("dop", "rng"), P())
    out_specs = P("dop", None, None, "rng")
    return jax.shard_map(body, mesh=mesh, in_specs=in_specs, out_specs=out_specs, check_vma=False)
```

profile of v0, /device:TPU:14, one launch (start us, length us, event | category | flops | bytes accessed | tf_op | source)
XLA Modules:
  0.0 496.1 jit_solution(3018158604492241891)
XLA Ops:
  6.8 0.9 copy-done
  7.8 0.9 fusion.15
  9.1 3.5 copy.87
  12.6 2.7 reshape.228
  15.3 4.0 all-to-all-start
  19.3 12.8 %all-to-all-done = bf16[4,2,65536]{2,1,0:T(2,128)(2,1)S(1)} async-done(((bf16[4,2,65536]{2,1,0:T(2,128)(2,1)}), bf16[4,2,65536]{2,1,0:T(2,128)(2,1)S(1)}, u32[]{:S(2)}, u32[]{:S(2)}) %all-to-all-start) | async-done | bytes 1048608 | tf_op jit(solution)/shard_map/all_to_all | solution.py:100
  32.0 1.4 reshape.229
  33.5 2.5 copy.89
  36.0 3.5 all_to_all.16
  39.8 2.1 collective-permute-start.1
  41.8 0.4 fusion.5
  42.3 2.5 stack.53
  44.8 0.4 fusion.11
  45.2 2.5 stack.50
  47.7 0.4 fusion.9
  48.1 1.2 copy-done.6
  49.3 1.5 constant_dynamic-update-slice_fusion.5
  50.8 2.5 stack.51
  53.2 0.4 fusion.7
  53.7 2.5 stack.52
  56.1 0.4 fusion.3
  56.6 2.5 stack.54
  59.1 0.4 fusion.1
  59.5 2.5 stack.55
  62.0 3.3 constant_dynamic-update-slice_fusion.4
  65.3 1.5 constant_dynamic-update-slice_fusion.3
  66.8 1.5 constant_dynamic-update-slice_fusion.2
  68.3 1.5 constant_dynamic-update-slice_fusion.1
  69.8 1.5 constant_dynamic-update-slice_fusion
  71.3 11.2 %fusion.55 = (f32[32,6,1,32,2,32]{5,4,3,2,0,1:T(2,128)}, f32[32,6,1,32,2,32]{5,4,3,2,0,1:T(2,128)}) fusion(f32[32,6,2,32,2,32]{5,4,3,2,0,1:T(2,128)} %constant_dynamic-update-slice_fusion), kind=kLoop, calls=%fused_computation.130 | loop fusion | bytes 6291456 | tf_op jit(solution)/shard_map/slice | solution.py:121
  82.5 10.7 %copy.143 = f32[32,6,1,32,2,32]{5,4,3,1,0,2:T(2,128)} copy(f32[32,6,1,32,2,32]{5,4,3,2,0,1:T(2,128)} %get-tuple-element.25) | data formatting | bytes 3145728
  93.2 39.3 %rev.3 = f32[32,6,32,2,32]{4,3,2,1,0:T(2,128)} reverse(f32[32,6,32,2,32]{4,3,2,1,0:T(2,128)} %bitcast.98), dimensions={3} | reverse | bytes 3145728 | tf_op jit(solution)/shard_map/rev | solution.py:121
  132.5 16.2 %fusion = f32[32,6,32,2,32]{4,3,2,1,0:T(2,128)} fusion(f32[32,6,1,32,2,32]{5,4,3,2,0,1:T(2,128)} %get-tuple-element.26, f32[32,6,32,2,32]{4,3,2,1,0:T(2,128)} %rev.3, f32[2]{0:T(128)S(1)} %copy-done.18), kind=kLoop, calls=%fused_computation.2 | loop fusion | flops 786432 | bytes 4718600 | tf_op jit(solution)/shard_map/add | solution.py:121
  148.7 7.1 %reshape.187 = f32[32,192,64]{2,1,0:T(8,128)} reshape(f32[32,6,32,2,32]{4,3,2,1,0:T(2,128)} %fusion) | data formatting | bytes 3145728 | tf_op jit(solution)/shard_map/reshape | solution.py:123
  156.2 0.7 copy.106
  157.0 0.6 iota_compare_fusion.6
  157.6 0.6 iota_compare_fusion.3
  158.2 0.6 iota_compare_fusion.1
  158.9 0.6 iota_compare_fusion.2
  159.5 0.6 pad_convert_fusion
  160.1 71.0 %reduce-scatter.2.cloned.1.call-done = f32[4,192,64]{2,1,0:T(8,128)} async-done(((f32[32,192,64]{2,1,0:T(8,128)}), f32[4,192,64]{2,1,0:T(8,128)}) %reduce-scatter.2.cloned.1.call-update) | async-done | bytes 196624 | tf_op jit(solution)/shard_map/reduce_scatter | solution.py:122
  231.2 1.5 reshape.188
  232.7 0.8 slice_negate_fusion
  233.5 0.9 maximum_bitcast_fusion
  234.5 0.5 stack_reshape.3
  234.9 0.8 pad_maximum_fusion
  235.8 1.2 copy.97
  237.0 2.3 reshape.189
  241.1 0.9 copy-done.7
  242.0 46.9 %custom-call.18 = f32[4,128,128]{2,1,0:T(8,128)S(1)} custom-call(f32[4,128,128]{2,1,0:T(8,128)S(1)} %cholesky.126), custom_call_target="Cholesky" | custom-call | tf_op jit(solution)/shard_map/jit(cholesky)/cholesky | solution.py:81
  289.0 39.3 %custom-call.19 = f32[4,1,128,128]{2,3,1,0:T(8,128)S(1)} custom-call(f32[4,1,128,128]{3,2,1,0:T(8,128)S(1)} %get-tuple-element.43), custom_call_target="InvertDiagBlocksLowerTriangular" | custom-call | tf_op jit(solution)/shard_map/jit(cholesky)/cholesky | solution.py:81
  328.3 1.3 constant_dynamic-update-slice_fusion.7
  329.6 1.3 convolution_subtract_fusion.2
  330.9 23.5 %custom-call.20 = f32[4,64,64]{2,1,0:T(8,128)S(1)} custom-call(f32[4,64,64]{2,1,0:T(8,128)S(1)} %convolution_subtract_fusion.2), custom_call_target="Cholesky" | custom-call | tf_op jit(solution)/shard_map/jit(cholesky)/cholesky | solution.py:81
  354.3 0.7 select_reduce_fusion.2
  355.3 1.0 select_select_fusion
  356.5 78.8 %custom-call.21 = f32[4,2,128,128]{2,3,1,0:T(8,128)S(1)} custom-call(f32[4,2,128,128]{3,2,1,0:T(8,128)S(1)} %pad_maximum_fusion.4), custom_call_target="InvertDiagBlocksLowerTriangular" | custom-call | tf_op jit(solution)/shard_map/triangular_solve | solution.py:84
  435.4 1.1 fusion.31
  437.8 0.6 fusion.30
  439.2 0.8 copy.115
  440.1 43.4 %all-gather.2.cloned.1.call-done = bf16[32,192,128]{2,1,0:T(8,128)(2,1)} async-done(((bf16[4,192,128]{2,1,0:T(8,128)(2,1)}), bf16[32,192,128]{2,1,0:T(8,128)(2,1)}) %all-gather.2.cloned.1.call-update) | async-done | bytes 1572880 | tf_op jit(solution)/shard_map/all_gather | solution.py:125
  483.5 1.9 fusion.19
  485.5 0.8 fusion.20
  486.2 2.8 add_add_fusion
  (97 shorter events, 5.8 us)
Async XLA Ops:
  6.5 1.2 copy-start
  9.1 10.2 %copy-start.17 = (s32[32,256]{1,0:T(8,128)S(1)}, s32[32,256]{1,0:T(8,128)}, u32[]{:S(2)}) copy-start(s32[32,256]{1,0:T(8,128)} %param.5) | copy-start | bytes 98308
  15.3 16.8 %all-to-all-start = ((bf16[4,2,65536]{2,1,0:T(2,128)(2,1)}), bf16[4,2,65536]{2,1,0:T(2,128)(2,1)S(1)}, u32[]{:S(2)}, u32[]{:S(2)}) async-start(bf16[4,2,65536]{2,1,0:T(2,128)(2,1)} %reshape.228), calls=%async_computation | async-start | bytes 2097152 | tf_op jit(solution)/shard_map/all_to_all | solution.py:100
  19.2 211.9 %reduce-scatter.2.cloned.1.call-start = ((), (), s32[]{:S(2)}) async-start(), calls=%async_computation.2 | async-start | bytes 3538944 | tf_op jit(solution)/shard_map/reduce_scatter | solution.py:122
  39.6 5.2 %collective-permute-start = (bf16[1,256,64]{1,2,0:T(8,128)(2,1)S(1)}, bf16[1,256,64]{1,2,0:T(8,128)(2,1)S(1)}, u32[]{:S(2)}, u32[]{:S(2)}) collective-permute-start(bf16[1,256,64]{1,2,0:T(8,128)(2,1)S(1)} %copy.126), channel_id=1, source_target_pairs={{0,8},{8,16},{16,24},{24,0},{1,9},{9,17},{17,25},{25,1},{2,10},{10... | collective-permute-start | bytes 98312 | tf_op jit(solution)/shard_map/ppermute | solution.py:24
  39.8 13.5 %collective-permute-start.1 = (bf16[1,256,64]{1,2,0:T(8,128)(2,1)S(1)}, bf16[1,256,64]{1,2,0:T(8,128)(2,1)S(1)}, u32[]{:S(2)}, u32[]{:S(2)}) collective-permute-start(bf16[1,256,64]{1,2,0:T(8,128)(2,1)S(1)} %copy.127), channel_id=1, source_target_pairs={{8,0},{16,8},{24,16},{0,24},{9,1},{17,9},{25,17},{1,25},{10,2},{18... | collective-permute-start | bytes 98312 | tf_op jit(solution)/shard_map/ppermute | solution.py:27
  44.8 8.5 %copy-start.13 = (bf16[1,256,64]{1,2,0:T(8,128)(2,1)}, bf16[1,256,64]{1,2,0:T(8,128)(2,1)S(1)}, u32[]{:S(2)}) copy-start(bf16[1,256,64]{1,2,0:T(8,128)(2,1)S(1)} %collective-permute-done) | copy-start | bytes 98308
  47.7 1.6 copy-start.6
  53.2 5.8 %copy-start.15 = (bf16[1,256,64]{1,2,0:T(8,128)(2,1)}, bf16[1,256,64]{1,2,0:T(8,128)(2,1)S(1)}, u32[]{:S(2)}) copy-start(bf16[1,256,64]{1,2,0:T(8,128)(2,1)S(1)} %collective-permute-done.1) | copy-start | bytes 98308
  62.0 3.3 copy-start.5
  62.0 4.8 copy-start.2
  65.3 3.0 copy-start.3
  66.8 3.0 copy-start.4
  93.2 39.3 %copy-start.18 = (f32[2]{0:T(128)S(1)}, f32[2]{0:T(128)}, u32[]{:S(2)}) copy-start(f32[2]{0:T(128)} %constant.143.clone) | copy-start | bytes 28
  148.7 7.4 %copy-start.19 = (s32[64]{0:T(128)S(1)}, s32[64]{0:T(128)}, u32[]{:S(2)}) copy-start(s32[64]{0:T(128)} %param.6) | copy-start | bytes 772
  155.8 327.7 %all-gather.2.cloned.1.call-start = ((), (), s32[]{:S(2)}) async-start(), calls=%async_computation.3 | async-start | bytes 1769472 | tf_op jit(solution)/shard_map/all_gather | solution.py:125
  231.2 3.3 copy-start.9
  235.8 4.3 copy-start.11
  240.1 48.9 %copy-start.12 = (pred[128,128]{1,0:T(8,128)(4,1)S(1)}, pred[128,128]{1,0:T(8,128)(4,1)}, u32[]{:S(2)}) copy-start(pred[128,128]{1,0:T(8,128)(4,1)} %get-tuple-element.53) | copy-start | bytes 49156
  241.0 115.4 %copy-start.10 = (f32[128,64]{1,0:T(8,128)S(1)}, f32[128,64]{1,0:T(8,128)}, u32[]{:S(2)}) copy-start(f32[128,64]{1,0:T(8,128)} %pad_convert_fusion) | copy-start | bytes 98308
  241.1 0.9 copy-start.7
  438.9 46.5 %copy-start.14 = (bf16[1,256,64]{1,2,0:T(8,128)(2,1)S(1)}, bf16[1,256,64]{1,2,0:T(8,128)(2,1)}, u32[]{:S(2)}) copy-start(bf16[1,256,64]{1,2,0:T(8,128)(2,1)} %copy-done.13) | copy-start | bytes 98308
  483.5 1.9 copy-start.8
  485.4 0.8 copy-start.16
  485.4 3.6 copy-start.1
Sparse Core Ops, SparseCore 0:
  155.9 75.2 reduce-scatter.1
  440.2 43.2 all-gather.1
where the time goes:
time: 505 us; the launch traced here: 496 us
  other arithmetic  214 us (42%)
  waiting for transfers between devices  127 us (25%)
  local copies, waits for them, and re-layouts  119 us (24%)
  matrix products  14.4 us (3%)
  between operations  14.3 us (3%)
  starting transfers between devices  6.34 us (1%)
    another operation x10, other arithmetic, mvdr_weights(): factor = jnp.linalg.cholesky(regular)  112 us
    another operation x7, other arithmetic, mvdr_weights(): lax.linalg.triangular_solve(factor, forward, left_side=True, lower=True,...  81.2 us
    reduce_scatter x1, waiting for transfers between devices, body(): lax.psum_scatter(upper_half.reshape(bin_count, 6 * CH, 2 * CH), 'rng', sc...  71 us
    all_gather x1, waiting for transfers between devices, body(): lax.all_gather(mvdr_weights(my_gram, steer), 'rng', axis=0, tiled=True)  43.4 us
    rev x1, local copies, waits for them, and re-layouts, body(): gram_blocks[:, :, 1][:, :, :, ::-1, :]  39.3 us
    unnamed x51, local copies, waits for them, and re-layouts  27.4 us
    another operation x7, local copies, waits for them, and re-layouts, body(): jnp.stack(products, axis=1).reshape(bin_count, 6, 2, CH, 2, CH)  16.4 us
    add x1, other arithmetic, body(): gram_blocks[:, :, 0] + flip_sign * gram_blocks[:, :, 1][:, :, :, ::-1, :]  16.2 us
  transfers between devices with their start and end apart: 5, of which 3 were waited for; matrix products, arithmetic and copies ran while one was open for 3% of the time, Pallas kernels for 0%

commit v1 on v0

v1 whole, which is shorter than its diff:
```python
import functools

import jax
import jax.numpy as jnp
import numpy as np
from jax import lax
from jax.experimental import pallas as pl
from jax.experimental.pallas import tpu as pltpu
from jax.sharding import PartitionSpec as P

CH = 32
PULSES = 128
LOOKS = 64
ANGLES = 256

loading = 0.1
epsilon = 1e-06
highest = lax.Precision.HIGHEST
MESH = pl.DeviceIdType.MESH
bf16 = jnp.bfloat16
f32 = jnp.float32


def twiddle_table():
    pulse_ids = np.arange(PULSES)
    bins = np.arange(-1, PULSES + 1) % PULSES
    angles = ((bins[:, None] * pulse_ids[None, :]) % PULSES).astype(np.float32) * np.float32(
        2.0 * np.pi / PULSES
    )
    cosine, sine = np.cos(angles), np.sin(angles)
    table = np.stack([np.stack([cosine, sine], 1), np.stack([-sine, cosine], 1)], 0)
    return jnp.asarray(table, bf16)


def steering(look_index):
    sines = -1.0 + (2.0 * look_index.astype(f32) + 1.0) / ANGLES
    channel_ids = jnp.arange(CH).astype(f32)
    phases = jnp.pi * channel_ids[:, None] * sines[None, :]
    return jnp.concatenate([jnp.cos(phases), jnp.sin(phases)], axis=0)


def exchange_kernel(D, R, spec, mask, wide, mine, masks, send_m, recv_m, send_x, recv_x,
                    send_w, recv_w, own):
    N = D * R
    bins = PULSES // D
    share = bins // R
    d, g = lax.axis_index("dop"), lax.axis_index("rng")
    me = g * D + d
    barrier = pltpu.get_barrier_semaphore()

    def where(j):
        t = lax.rem(me + j, N)
        return t, lax.rem(t, D), t // D

    def greet(j, c):
        _, td, tg = where(j)
        pl.semaphore_signal(barrier, inc=1, device_id=(td, tg), device_id_type=MESH)
        return c

    lax.fori_loop(1, N, greet, 0)
    local = [
        pltpu.make_async_copy(mask.at[g], masks.at[g], own.at[0]),
        pltpu.make_async_copy(spec.at[pl.ds(d * bins + g * share, share + 2)], mine.at[me], own.at[1]),
        pltpu.make_async_copy(spec.at[pl.ds(d * bins, bins + 2)], wide.at[d], own.at[2]),
    ]
    for copy in local:
        copy.start()
    pl.semaphore_wait(barrier, N - 1)

    def mask_copy(j):
        tg = lax.rem(g + j, R)
        return pltpu.make_async_remote_copy(
            mask.at[tg], masks.at[g], send_m.at[j], recv_m.at[g], device_id=(d, tg),
            device_id_type=MESH)

    def mine_copy(j):
        _, td, tg = where(j)
        return pltpu.make_async_remote_copy(
            spec.at[pl.ds(td * bins + tg * share, share + 2)], mine.at[me], send_x.at[j],
            recv_x.at[me], device_id=(td, tg), device_id_type=MESH)

    def wide_copy(j):
        td = lax.rem(d + j, D)
        return pltpu.make_async_remote_copy(
            spec.at[pl.ds(td * bins, bins + 2)], wide.at[d], send_w.at[j], recv_w.at[d],
            device_id=(td, g), device_id_type=MESH)

    def start(make):
        def run(j, c):
            make(j).start()
            return c
        return run

    lax.fori_loop(1, R, start(mask_copy), 0)
    lax.fori_loop(1, N, start(mine_copy), 0)
    lax.fori_loop(1, D, start(wide_copy), 0)

    def end_mask(j, c):
        src = lax.rem(g + j, R)
        mask_copy(j).wait_send()
        pltpu.make_async_remote_copy(
            mask.at[0], masks.at[src], send_m.at[j], recv_m.at[src], device_id=(d, src),
            device_id_type=MESH).wait_recv()
        return c

    def end_mine(j, c):
        src, sd, sg = where(j)
        mine_copy(j).wait_send()
        pltpu.make_async_remote_copy(
            spec.at[pl.ds(0, share + 2)], mine.at[src], send_x.at[j], recv_x.at[src],
            device_id=(sd, sg), device_id_type=MESH).wait_recv()
        return c

    def end_wide(j, c):
        src = lax.rem(d + j, D)
        wide_copy(j).wait_send()
        pltpu.make_async_remote_copy(
            spec.at[pl.ds(0, bins + 2)], wide.at[src], send_w.at[j], recv_w.at[src],
            device_id=(src, g), device_id_type=MESH).wait_recv()
        return c

    lax.fori_loop(1, R, end_mask, 0)
    lax.fori_loop(1, N, end_mine, 0)
    lax.fori_loop(1, D, end_wide, 0)
    for copy in local:
        copy.wait()


def gather_kernel(R, unit, out, send, recv, own):
    d, g = lax.axis_index("dop"), lax.axis_index("rng")
    barrier = pltpu.get_barrier_semaphore()

    def greet(j, c):
        pl.semaphore_signal(barrier, inc=1, device_id=(d, lax.rem(g + j, R)), device_id_type=MESH)
        return c

    lax.fori_loop(1, R, greet, 0)
    local = pltpu.make_async_copy(unit, out.at[g], own)
    local.start()
    pl.semaphore_wait(barrier, R - 1)

    def make(j):
        tg = lax.rem(g + j, R)
        return pltpu.make_async_remote_copy(
            unit, out.at[g], send.at[j], recv.at[g], device_id=(d, tg), device_id_type=MESH)

    def begin(j, c):
        make(j).start()
        return c

    def end(j, c):
        src = lax.rem(g + j, R)
        make(j).wait_send()
        pltpu.make_async_remote_copy(
            unit, out.at[src], send.at[j], recv.at[src], device_id=(d, src),
            device_id_type=MESH).wait_recv()
        return c

    lax.fori_loop(1, R, begin, 0)
    lax.fori_loop(1, R, end, 0)
    local.wait()


def invert(re, im):
    width = re.shape[1]
    lane = lax.broadcasted_iota(jnp.int32, (CH, width), 1)
    row = lax.broadcasted_iota(jnp.int32, (CH, width), 0)
    base = lane // CH * CH
    col = lane - base
    for k in range(CH):
        pick = base + k
        cr = jnp.take_along_axis(re, pick, axis=1)
        ci = jnp.take_along_axis(im, pick, axis=1)
        at_col, at_row = col == k, row == k
        scale = 1.0 / cr[k:k + 1]
        rr = jnp.where(at_col[:1], 1.0, re[k:k + 1]) * scale
        ri = jnp.where(at_col[:1], 0.0, im[k:k + 1]) * scale
        clear = jnp.logical_or(at_col, at_row)
        cr = jnp.where(at_row, -1.0, cr)
        ci = jnp.where(at_row, 0.0, ci)
        re = jnp.where(clear, 0.0, re) - (cr * rr - ci * ri)
        im = jnp.where(clear, 0.0, im) - (cr * ri + ci * rr)
    return re, im


def stacked_form(re, im):
    return jnp.concatenate([re, im], axis=0)


def full_form(stacked):
    re, im = stacked[:CH], stacked[CH:]
    return jnp.concatenate(
        [jnp.concatenate([re, -im], axis=1), jnp.concatenate([im, re], axis=1)], axis=0)


def mul(a, b):
    return jnp.dot(a, b, precision=highest, preferred_element_type=f32)


def invert_all(blocks):
    lanes = 128 // CH
    packed = (blocks * lanes)[:lanes] if len(blocks) < lanes else blocks
    re, im = invert(
        jnp.concatenate([block[:CH] for block in packed], axis=1),
        jnp.concatenate([block[CH:] for block in packed], axis=1))
    return [
        stacked_form(re[:, i * CH:(i + 1) * CH], im[:, i * CH:(i + 1) * CH])
        for i in range(len(blocks))
    ]


def weights_kernel(D, R, share, mine, masks, steer, unit, gram):
    lane = lax.broadcasted_iota(jnp.int32, (CH, 128), 1)
    sign = jnp.where(lane < 64, -1.0, 1.0).astype(bf16)
    gram[...] = jnp.zeros_like(gram)

    def add(g, c):
        rows = masks[g].astype(f32)
        plain = [[mine[g * D + s, b] for s in range(D)] for b in range(share + 2)]
        turned = [[pltpu.roll(x.astype(f32), 64, 1).astype(bf16) * sign for x in line] for line in plain]
        plain_k = [jnp.concatenate(line, axis=1) for line in plain]
        turned_k = [jnp.concatenate(line, axis=1) for line in turned]
        for b in range(share):
            weight = jnp.concatenate(
                [jnp.broadcast_to(rows[b * D + s:b * D + s + 1], (CH, 128)).astype(bf16)
                 for s in range(D)], axis=1)
            left = jnp.concatenate([plain_k[b + i] * weight for i in range(3)], axis=0)
            right = jnp.concatenate(
                [plain_k[b + i] for i in range(3)] + [turned_k[b + i] for i in range(3)], axis=0)
            gram[b] += lax.dot_general(
                left, right, (((1,), (1,)), ((), ())), preferred_element_type=f32)
        return c

    lax.fori_loop(0, R, add, 0)

    eye_r = lax.broadcasted_iota(jnp.int32, (3 * CH, 6 * CH), 0)
    eye_c = lax.broadcasted_iota(jnp.int32, (3 * CH, 6 * CH), 1)
    diagonal = eye_r == eye_c
    cov = []
    for b in range(share):
        whole = gram[b]
        trace = jnp.sum(jnp.where(diagonal, whole, 0.0), keepdims=True)
        power = trace / (3 * CH) + epsilon
        whole = whole / power + jnp.where(diagonal, loading, 0.0)
        cov.append([[
            stacked_form(whole[i * CH:(i + 1) * CH, j * CH:(j + 1) * CH],
                         whole[i * CH:(i + 1) * CH, (3 + j) * CH:(4 + j) * CH])
            for j in range(3)] for i in range(3)])
    every = range(share)
    inverse0 = invert_all([cov[b][0][0] for b in every])
    ahead = [mul(full_form(inverse0[b]), jnp.concatenate([cov[b][0][1], cov[b][0][2]], axis=1))
             for b in every]
    down = [mul(jnp.concatenate([full_form(cov[b][1][0]), full_form(cov[b][2][0])], axis=0), ahead[b])
            for b in every]
    c11 = [cov[b][1][1] - down[b][:2 * CH, :CH] for b in every]
    c12 = [cov[b][1][2] - down[b][:2 * CH, CH:] for b in every]
    c21 = [cov[b][2][1] - down[b][2 * CH:, :CH] for b in every]
    inverse2 = invert_all([cov[b][2][2] - down[b][2 * CH:, CH:] for b in every])
    back = [mul(full_form(inverse2[b]), c21[b]) for b in every]
    inverse1 = invert_all([c11[b] - mul(full_form(c12[b]), back[b]) for b in every])
    steer_here = steer[...]
    for b in every:
        x1 = mul(full_form(inverse1[b]), steer_here)
        x2 = -mul(full_form(back[b]), x1)
        x0 = -(mul(full_form(ahead[b][:, :CH]), x1) + mul(full_form(ahead[b][:, CH:]), x2))
        gain = jnp.sum(steer_here * x1, axis=0, keepdims=True)
        scale = 1.0 / jnp.sqrt(gain)
        parts = [x * scale for x in (x0, x1, x2)]
        unit[b] = jnp.concatenate(
            [jnp.concatenate([x[:CH], x[CH:]], axis=1) for x in parts], axis=0).astype(bf16)


def beams_kernel(D, step_bins, wide, unit, out):
    first = pl.program_id(0) * step_bins
    lane = lax.broadcasted_iota(jnp.int32, (CH, 128), 1)
    sign = jnp.where(lane < 64, 1.0, -1.0).astype(bf16)
    rows = []
    for b in range(step_bins + 2):
        pieces = [wide[s, first + b] for s in range(D)]
        rows.append(jnp.concatenate([x[:, :64] for x in pieces], axis=1))
        rows.append(jnp.concatenate([x[:, 64:] for x in pieces], axis=1))
    for b in range(step_bins):
        weight = []
        for i in range(3):
            u = unit[b, i * CH:(i + 1) * CH]
            weight.append(u * sign)
            weight.append(pltpu.roll(u.astype(f32), 64, 1).astype(bf16))
        out[b] = lax.dot_general(
            jnp.concatenate(weight, axis=0), jnp.concatenate(rows[2 * b:2 * b + 6], axis=0),
            (((0,), (0,)), ((), ())), preferred_element_type=f32)


def body(echoes, training, look_index):
    D, R = lax.axis_size("dop"), lax.axis_size("rng")
    N = D * R
    bins = PULSES // D
    share = bins // R
    cells = echoes.shape[0]
    spec = jnp.einsum("qkQp,rQcp->kcqr", twiddle_table(), echoes, preferred_element_type=f32)
    spec = spec.astype(bf16).reshape(PULSES + 2, CH, 2 * cells)
    mask = training.astype(bf16).reshape(R, share, D, 1, cells)
    mask = jnp.broadcast_to(mask, (R, share, D, 2, cells)).reshape(R, share * D, 2 * cells)
    mask = jnp.pad(mask, ((0, 0), (0, -share * D % 16), (0, 0)))
    steer = steering(look_index)
    anywhere = pl.BlockSpec(memory_space=pl.ANY)
    in_vmem = pl.BlockSpec(memory_space=pltpu.VMEM)
    dma = pltpu.SemaphoreType.DMA
    wide, mine, masks = pl.pallas_call(
        functools.partial(exchange_kernel, D, R),
        out_shape=[
            jax.ShapeDtypeStruct((D, bins + 2, CH, 2 * cells), bf16),
            jax.ShapeDtypeStruct((N, share + 2, CH, 2 * cells), bf16),
            jax.ShapeDtypeStruct(mask.shape, bf16),
        ],
        in_specs=[anywhere] * 2,
        out_specs=[anywhere] * 3,
        scratch_shapes=[dma((R,)), dma((R,)), dma((N,)), dma((N,)), dma((D,)), dma((D,)), dma((3,))],
        compiler_params=pltpu.CompilerParams(collective_id=0, has_side_effects=True),
        name="exchange",
    )(spec, mask)
    unit = pl.pallas_call(
        functools.partial(weights_kernel, D, R, share),
        out_shape=jax.ShapeDtypeStruct((share, 3 * CH, 2 * LOOKS), bf16),
        in_specs=[in_vmem] * 3,
        out_specs=in_vmem,
        scratch_shapes=[pltpu.VMEM((share, 3 * CH, 6 * CH), f32)],
        compiler_params=pltpu.CompilerParams(vmem_limit_bytes=32 * 1024 * 1024),
        name="weights",
    )(mine, masks, steer)
    units = pl.pallas_call(
        functools.partial(gather_kernel, R),
        out_shape=jax.ShapeDtypeStruct((R,) + unit.shape, bf16),
        in_specs=[anywhere],
        out_specs=anywhere,
        scratch_shapes=[dma((R,)), dma((R,)), dma],
        compiler_params=pltpu.CompilerParams(collective_id=1, has_side_effects=True),
        name="gather",
    )(unit)
    units = units.reshape(bins, 3 * CH, 2 * LOOKS)
    step_bins = 4
    out = pl.pallas_call(
        functools.partial(beams_kernel, D, step_bins),
        grid=(bins // step_bins,),
        out_shape=jax.ShapeDtypeStruct((bins, 2 * LOOKS, D * cells), f32),
        in_specs=[
            in_vmem,
            pl.BlockSpec((step_bins, 3 * CH, 2 * LOOKS), lambda i: (i, 0, 0)),
        ],
        out_specs=pl.BlockSpec((step_bins, 2 * LOOKS, D * cells), lambda i: (i, 0, 0)),
        compiler_params=pltpu.CompilerParams(vmem_limit_bytes=32 * 1024 * 1024),
        name="beams",
    )(wide, units)
    return out.reshape(bins, 2, LOOKS, D * cells)


def solution(mesh):
    in_specs = (P(("rng", "dop"), None, None, None), P("dop", "rng"), P())
    out_specs = P("dop", None, None, "rng")
    return jax.shard_map(body, mesh=mesh, in_specs=in_specs, out_specs=out_specs, check_vma=False)
```

time: 505 us -> 103 us (0.20); the launches traced: 496 us -> 102 us
  other arithmetic: 214 us -> 1.57 us
  waiting for transfers between devices: 127 us -> 0 us
  local copies, waits for them, and re-layouts: 119 us -> 12 us
  Pallas kernels: 0 us -> 85.1 us
  between operations: 14.3 us -> 0.08 us
  matrix products: 14.4 us -> 3.56 us
  starting transfers between devices: 6.34 us -> 0 us
    another operation x27 -> x0, other arithmetic: 196 us -> none  [the longest x10 112 us: mvdr_weights(): factor = jnp.linalg.cholesky(regular)]
    pallas_call x0 -> x4, Pallas kernels: none -> 85.1 us  [the longest x1 43 us: body(): pl.pallas_call(functools.partial(exchange_kernel, D, R), out_shape=[jax.S...]
    reduce_scatter x1 -> x0, waiting for transfers between devices: 71 us -> none  [body(): lax.psum_scatter(upper_half.reshape(bin_count, 6 * CH, 2 * CH), 'rng', sc...]
    all_gather x1 -> x0, waiting for transfers between devices: 43.4 us -> none  [body(): lax.all_gather(mvdr_weights(my_gram, steer), 'rng', axis=0, tiled=True)]
    rev x1 -> x0, local copies, waits for them, and re-layouts: 39.3 us -> none  [body(): gram_blocks[:, :, 1][:, :, :, ::-1, :]]
    unnamed x51 -> x10, local copies, waits for them, and re-layouts: 27.4 us -> 3.94 us
    another operation x17 -> x0, local copies, waits for them, and re-layouts: 19.1 us -> none  [the longest x7 16.4 us: body(): jnp.stack(products, axis=1).reshape(bin_count, 6, 2, CH, 2, CH)]
    add x4 -> x1, other arithmetic: 16.4 us -> 0.66 us  [steering(): sines = -1.0 + (2.0 * look_index.astype(f32) + 1.0) / ANGLES]
  transfers between devices with their start and end apart: 5 -> 0, of which waited for: 3 -> 0; matrix products, arithmetic and copies ran while one was open for 3% -> 0% of each run, Pallas kernels for 0% -> 0%
where the time goes in v1:
time: 103 us; the launch traced here: 102 us
  Pallas kernels  85.1 us (83%)
  local copies, waits for them, and re-layouts  12 us (12%)
  matrix products  3.56 us (3%)
  other arithmetic  1.57 us (2%)
    pallas_call x1, Pallas kernels, body(): pl.pallas_call(functools.partial(exchange_kernel, D, R), out_shape=[jax.S...  43 us
    pallas_call x1, Pallas kernels, body(): pl.pallas_call(functools.partial(gather_kernel, R), out_shape=jax.ShapeDt...  21.8 us
    pallas_call x1, Pallas kernels, body(): pl.pallas_call(functools.partial(weights_kernel, D, R, share), out_shape=...  15 us
    convert_element_type x1, local copies, waits for them, and re-layouts, body(): spec = spec.astype(bf16).reshape(PULSES + 2, CH, 2 * cells)  5.42 us
    pallas_call x1, Pallas kernels, body(): pl.pallas_call(functools.partial(beams_kernel, D, step_bins), grid=(bins...  5.33 us
    unnamed x10, local copies, waits for them, and re-layouts  3.94 us
    dot_general x1, matrix products, body(): jnp.einsum('qkQp,rQcp->kcqr', twiddle_table(), echoes, preferred_element_...  3.56 us

profile of v1, /device:TPU:14, one launch (start us, length us, event | category | flops | bytes accessed | tf_op | source)
XLA Modules:
  0.0 102.3 jit_solution(874750642160080716)
XLA Ops:
  0.0 0.7 multiply_add_fusion
  0.7 0.8 convert_element_type.21
  1.4 0.1 broadcast_in_dim.4
  1.5 0.1 multiply_cosine_fusion
  1.7 0.7 reshape.22.mask
  2.4 3.6 %fusion = bf16[130,32,2,64]{0,3,1,2:T(8,128)(2,1)} fusion(bf16[2,130,2,128,1]{3,1,2,4,0:T(8,128)(2,1)} %constant.15, bf16[64,2,32,128]{3,2,1,0:T(8,128)(2,1)} %param.4), kind=kOutput, calls=%fused_computation.1 | convolution fusion | flops 273162240 | bytes 2246656 | tf_op jit(solution)/shard_map/qkQp,rQcp->kcqr/dot_general | solution.py:299
  6.0 5.4 %copy.8 = bf16[130,32,2,64]{3,2,1,0:T(2,128)(2,1)S(1)} copy(bf16[130,32,2,64]{0,3,1,2:T(8,128)(2,1)} %fusion) | data formatting | bytes 2129920 | tf_op jit(solution)/shard_map/convert_element_type | solution.py:300
  11.4 1.8 %reshape.21.spec = bf16[130,32,128]{2,1,0:T(8,128)(2,1)} reshape(bf16[130,32,2,64]{3,2,1,0:T(2,128)(2,1)S(1)} %copy.8) | data formatting | bytes 2129920 | tf_op jit(solution)/shard_map/reshape | solution.py:300
  13.2 43.0 %exchange.1 = (bf16[4,34,32,128]{3,2,1,0:T(8,128)(2,1)}, bf16[32,6,32,128]{3,2,1,0:T(8,128)(2,1)}, bf16[8,16,128]{2,1,0:T(8,128)(2,1)}) custom-call(bf16[130,32,128]{2,1,0:T(8,128)(2,1)} %reshape.21.spec, bf16[8,16,128]{2,1,0:T(8,128)(2,1)} %reshape.22.mask), custom_call_target="tpu_custom_call" | custom-call | tf_op jit(solution)/shard_map/exchange/pallas_call | solution.py:308
  56.2 0.0 copy-start.1
  56.2 1.4 %copy-done.1 = bf16[32,6,32,128]{3,2,1,0:T(8,128)(2,1)S(1)} copy-done((bf16[32,6,32,128]{3,2,1,0:T(8,128)(2,1)S(1)}, bf16[32,6,32,128]{3,2,1,0:T(8,128)(2,1)}, u32[]{:S(2)}) %copy-start.1) | copy-done | bytes 1572888
  57.6 0.0 copy-start.4
  57.6 0.8 copy-done.4
  58.4 0.0 copy-start.2
  58.4 15.0 %weights.1.unit = bf16[4,96,128]{2,1,0:T(8,128)(2,1)S(1)} custom-call(bf16[32,6,32,128]{3,2,1,0:T(8,128)(2,1)S(1)} %copy-done.1, bf16[8,16,128]{2,1,0:T(8,128)(2,1)S(1)} %copy-done.4, f32[64,64]{1,0:T(8,128)S(1)} %pad_maximum_fusion.steer), custom_call_target="tpu_custom_call" | custom-call | tf_op jit(solution)/shard_map/weights/pallas_call | solution.py:321
  73.4 0.0 copy-start.3
  73.4 0.6 copy-done.3
  74.0 21.8 %gather.1 = bf16[8,4,96,128]{3,2,1,0:T(8,128)(2,1)} custom-call(bf16[4,96,128]{2,1,0:T(8,128)(2,1)} %copy-done.3), custom_call_target="tpu_custom_call" | custom-call | tf_op jit(solution)/shard_map/gather/pallas_call | solution.py:330
  95.8 0.0 copy-done.2
  95.8 0.0 copy-start
  95.8 1.1 %copy-done = bf16[8,4,96,128]{3,2,1,0:T(8,128)(2,1)S(1)} copy-done((bf16[8,4,96,128]{3,2,1,0:T(8,128)(2,1)S(1)}, bf16[8,4,96,128]{3,2,1,0:T(8,128)(2,1)}, u32[]{:S(2)}) %copy-start) | copy-done | bytes 786456
  97.0 5.3 %beams.1 = f32[32,128,256]{2,1,0:T(8,128)} custom-call(bf16[4,34,32,128]{3,2,1,0:T(8,128)(2,1)S(1)} %copy-done.2, bf16[32,96,128]{2,1,0:T(8,128)(2,1)S(1)} %bitcast.16), custom_call_target="tpu_custom_call" | custom-call | tf_op jit(solution)/shard_map/beams/pallas_call | solution.py:341
  (3 shorter events, 0.1 us)
Async XLA Ops:
  56.2 1.4 %copy-start.1 = (bf16[32,6,32,128]{3,2,1,0:T(8,128)(2,1)S(1)}, bf16[32,6,32,128]{3,2,1,0:T(8,128)(2,1)}, u32[]{:S(2)}) copy-start(bf16[32,6,32,128]{3,2,1,0:T(8,128)(2,1)} %get-tuple-element.9.mine) | copy-start | bytes 4718596
  57.6 0.8 copy-start.4
  58.4 37.4 %copy-start.2 = (bf16[4,34,32,128]{3,2,1,0:T(8,128)(2,1)S(1)}, bf16[4,34,32,128]{3,2,1,0:T(8,128)(2,1)}, u32[]{:S(2)}) copy-start(bf16[4,34,32,128]{3,2,1,0:T(8,128)(2,1)} %get-tuple-element.8.wide) | copy-start | bytes 3342340
  73.4 0.6 copy-start.3
  95.8 1.1 %copy-start = (bf16[8,4,96,128]{3,2,1,0:T(8,128)(2,1)S(1)}, bf16[8,4,96,128]{3,2,1,0:T(8,128)(2,1)}, u32[]{:S(2)}) copy-start(bf16[8,4,96,128]{3,2,1,0:T(8,128)(2,1)} %gather.1) | copy-start | bytes 2359300

commit v2 on v1

--- a/solution.py
+++ b/solution.py
@@ -21,15 +21,31 @@
 f32 = jnp.float32
 
 
-def twiddle_table():
+def twiddle_table(rows):
     pulse_ids = np.arange(PULSES)
-    bins = np.arange(-1, PULSES + 1) % PULSES
+    bins = np.arange(-1, rows - 1) % PULSES
     angles = ((bins[:, None] * pulse_ids[None, :]) % PULSES).astype(np.float32) * np.float32(
         2.0 * np.pi / PULSES
     )
-    cosine, sine = np.cos(angles), np.sin(angles)
-    table = np.stack([np.stack([cosine, sine], 1), np.stack([-sine, cosine], 1)], 0)
-    return jnp.asarray(table, bf16)
+    return jnp.asarray(np.concatenate([np.cos(angles), np.sin(angles)], axis=1), bf16)
+
+
+def spectra_kernel(group, echoes, table, spec):
+    left = table[...]
+    for first in range(0, CH, group):
+        real, imag = [
+            jnp.swapaxes(echoes[:, q, first:first + group].astype(f32), 0, 1).astype(bf16)
+            for q in range(2)
+        ]
+        planes = []
+        for c in range(group):
+            right = jnp.concatenate(
+                [jnp.concatenate([real[c], imag[c]], axis=1),
+                 jnp.concatenate([imag[c], -real[c]], axis=1)], axis=0)
+            planes.append(lax.dot_general(
+                left, right, (((1,), (1,)), ((), ())), preferred_element_type=f32))
+        turned = jnp.swapaxes(jnp.stack(planes), 0, 1)
+        spec[:, first:first + group] = turned.astype(bf16)
 
 
 def steering(look_index):
@@ -126,38 +142,65 @@
         copy.wait()
 
 
-def gather_kernel(R, unit, out, send, recv, own):
+def gather_kernel(R, unit, out, send, recv, pass_on, own):
+    H = R // 2
     d, g = lax.axis_index("dop"), lax.axis_index("rng")
+    half = g // H * H
+    partner = lax.rem(g + H, R)
+    other = H - half
     barrier = pltpu.get_barrier_semaphore()
 
+    def peer(j):
+        return half + lax.rem(g - half + j, H)
+
     def greet(j, c):
-        pl.semaphore_signal(barrier, inc=1, device_id=(d, lax.rem(g + j, R)), device_id_type=MESH)
-        return c
-
-    lax.fori_loop(1, R, greet, 0)
+        pl.semaphore_signal(barrier, inc=1, device_id=(d, peer(j)), device_id_type=MESH)
+        return c
+
+    lax.fori_loop(1, H, greet, 0)
+    pl.semaphore_signal(barrier, inc=1, device_id=(d, partner), device_id_type=MESH)
     local = pltpu.make_async_copy(unit, out.at[g], own)
     local.start()
-    pl.semaphore_wait(barrier, R - 1)
+    pl.semaphore_wait(barrier, H)
+
+    cross = pltpu.make_async_remote_copy(
+        unit, out.at[g], send.at[0], recv.at[g], device_id=(d, partner), device_id_type=MESH)
+    cross.start()
 
     def make(j):
-        tg = lax.rem(g + j, R)
         return pltpu.make_async_remote_copy(
-            unit, out.at[g], send.at[j], recv.at[g], device_id=(d, tg), device_id_type=MESH)
+            unit, out.at[g], send.at[j], recv.at[g], device_id=(d, peer(j)), device_id_type=MESH)
+
+    def hand(j):
+        return pltpu.make_async_remote_copy(
+            out.at[partner], out.at[partner], pass_on.at[j], recv.at[partner],
+            device_id=(d, peer(j)), device_id_type=MESH)
+
+    def arrive(src):
+        pltpu.make_async_remote_copy(
+            unit, out.at[src], send.at[0], recv.at[src], device_id=(d, partner),
+            device_id_type=MESH).wait_recv()
 
     def begin(j, c):
         make(j).start()
         return c
 
+    def begin_hand(j, c):
+        hand(j).start()
+        return c
+
     def end(j, c):
-        src = lax.rem(g + j, R)
         make(j).wait_send()
-        pltpu.make_async_remote_copy(
-            unit, out.at[src], send.at[j], recv.at[src], device_id=(d, src),
-            device_id_type=MESH).wait_recv()
-        return c
-
-    lax.fori_loop(1, R, begin, 0)
-    lax.fori_loop(1, R, end, 0)
+        hand(j).wait_send()
+        arrive(peer(j))
+        arrive(other + lax.rem(g - half + j, H))
+        return c
+
+    lax.fori_loop(1, H, begin, 0)
+    arrive(partner)
+    lax.fori_loop(1, H, begin_hand, 0)
+    lax.fori_loop(1, H, end, 0)
+    cross.wait_send()
     local.wait()
 
 
@@ -296,8 +339,7 @@
     bins = PULSES // D
     share = bins // R
     cells = echoes.shape[0]
-    spec = jnp.einsum("qkQp,rQcp->kcqr", twiddle_table(), echoes, preferred_element_type=f32)
-    spec = spec.astype(bf16).reshape(PULSES + 2, CH, 2 * cells)
+    rows = PULSES + 8
     mask = training.astype(bf16).reshape(R, share, D, 1, cells)
     mask = jnp.broadcast_to(mask, (R, share, D, 2, cells)).reshape(R, share * D, 2 * cells)
     mask = jnp.pad(mask, ((0, 0), (0, -share * D % 16), (0, 0)))
@@ -305,6 +347,14 @@
     anywhere = pl.BlockSpec(memory_space=pl.ANY)
     in_vmem = pl.BlockSpec(memory_space=pltpu.VMEM)
     dma = pltpu.SemaphoreType.DMA
+    spec = pl.pallas_call(
+        functools.partial(spectra_kernel, 16),
+        out_shape=jax.ShapeDtypeStruct((rows, CH, 2 * cells), bf16),
+        in_specs=[in_vmem] * 2,
+        out_specs=in_vmem,
+        compiler_params=pltpu.CompilerParams(vmem_limit_bytes=32 * 1024 * 1024),
+        name="spectra",
+    )(echoes, twiddle_table(rows))
     wide, mine, masks = pl.pallas_call(
         functools.partial(exchange_kernel, D, R),
         out_shape=[
@@ -332,7 +382,7 @@
         out_shape=jax.ShapeDtypeStruct((R,) + unit.shape, bf16),
         in_specs=[anywhere],
         out_specs=anywhere,
-        scratch_shapes=[dma((R,)), dma((R,)), dma],
+        scratch_shapes=[dma((R,)), dma((R,)), dma((R,)), dma],
         compiler_params=pltpu.CompilerParams(collective_id=1, has_side_effects=True),
         name="gather",
     )(unit)

time: 103 us -> 90.7 us (0.88)
  Pallas kernels: 85.1 us -> 80.6 us
  local copies, waits for them, and re-layouts: 12 us -> 7.86 us
  matrix products: 3.56 us -> 0 us
    pallas_call x1, Pallas kernels: 21.8 us -> 15.9 us  [body(): pl.pallas_call(functools.partial(gather_kernel, R), out_shape=jax.ShapeDt...]
    convert_element_type x1 -> x0, local copies, waits for them, and re-layouts: 5.42 us -> none  [body(): spec = spec.astype(bf16).reshape(PULSES + 2, CH, 2 * cells)]
    dot_general x1 -> x0, matrix products: 3.56 us -> none  [body(): jnp.einsum('qkQp,rQcp->kcqr', twiddle_table(), echoes, preferred_element_...]
    unnamed x10 -> x16, local copies, waits for them, and re-layouts: 3.94 us -> 7.03 us
    reshape x1 -> x0, local copies, waits for them, and re-layouts: 1.79 us -> none  [body(): spec = spec.astype(bf16).reshape(PULSES + 2, CH, 2 * cells)]
    pallas_call x0 -> x1, Pallas kernels: none -> 1.3 us  [body(): pl.pallas_call(functools.partial(spectra_kernel, 16), out_shape=jax.Shape...]
where the time goes in v2:
time: 90.7 us; the launch traced here: 90.1 us
  Pallas kernels  80.6 us (89%)
  local copies, waits for them, and re-layouts  7.86 us (9%)
  other arithmetic  1.57 us (2%)
    pallas_call x1, Pallas kernels, body(): pl.pallas_call(functools.partial(exchange_kernel, D, R), out_shape=[jax.S...  43 us
    pallas_call x1, Pallas kernels, body(): pl.pallas_call(functools.partial(gather_kernel, R), out_shape=jax.ShapeDt...  15.9 us
    pallas_call x1, Pallas kernels, body(): pl.pallas_call(functools.partial(weights_kernel, D, R, share), out_shape=...  15 us
    unnamed x16, local copies, waits for them, and re-layouts  7.03 us
    pallas_call x1, Pallas kernels, body(): pl.pallas_call(functools.partial(beams_kernel, D, step_bins), grid=(bins...  5.33 us

profile of v2, /device:TPU:14, one launch (start us, length us, event | category | flops | bytes accessed | tf_op | source)
XLA Modules:
  0.0 90.1 jit_solution(15253068841343418307)
XLA Ops:
  0.0 0.7 multiply_add_fusion
  0.7 0.8 convert_element_type.13
  1.4 0.1 broadcast_in_dim.4
  1.5 0.1 multiply_cosine_fusion
  1.7 0.7 reshape.18.mask
  2.4 0.0 copy-start.4
  2.4 1.2 %copy-done.4 = bf16[64,2,32,128]{3,2,1,0:T(8,128)(2,1)S(1)} copy-done((bf16[64,2,32,128]{3,2,1,0:T(8,128)(2,1)S(1)}, bf16[64,2,32,128]{3,2,1,0:T(8,128)(2,1)}, u32[]{:S(2)}) %copy-start.4) | copy-done | bytes 1048600
  3.7 0.0 copy-start.6
  3.7 0.9 copy-done.6
  4.5 1.3 %spectra.1.spec = bf16[136,32,128]{2,1,0:T(8,128)(2,1)S(1)} custom-call(bf16[64,2,32,128]{3,2,1,0:T(8,128)(2,1)S(1)} %copy-done.4, bf16[136,256]{1,0:T(8,128)(2,1)S(1)} %copy-done.6), custom_call_target="tpu_custom_call" | custom-call | tf_op jit(solution)/shard_map/spectra/pallas_call | solution.py:350
  5.8 0.0 copy-start
  5.9 1.0 %copy-done = bf16[136,32,128]{2,1,0:T(8,128)(2,1)} copy-done((bf16[136,32,128]{2,1,0:T(8,128)(2,1)}, bf16[136,32,128]{2,1,0:T(8,128)(2,1)S(1)}, u32[]{:S(2)}) %copy-start) | copy-done | bytes 1114136
  6.8 43.0 %exchange.1 = (bf16[4,34,32,128]{3,2,1,0:T(8,128)(2,1)}, bf16[32,6,32,128]{3,2,1,0:T(8,128)(2,1)}, bf16[8,16,128]{2,1,0:T(8,128)(2,1)}) custom-call(bf16[136,32,128]{2,1,0:T(8,128)(2,1)} %copy-done, bf16[8,16,128]{2,1,0:T(8,128)(2,1)} %reshape.18.mask), custom_call_target="tpu_custom_call" | custom-call | tf_op jit(solution)/shard_map/exchange/pallas_call | solution.py:358
  49.9 0.0 copy-start.2
  49.9 1.4 %copy-done.2 = bf16[32,6,32,128]{3,2,1,0:T(8,128)(2,1)S(1)} copy-done((bf16[32,6,32,128]{3,2,1,0:T(8,128)(2,1)S(1)}, bf16[32,6,32,128]{3,2,1,0:T(8,128)(2,1)}, u32[]{:S(2)}) %copy-start.2) | copy-done | bytes 1572888
  51.3 0.0 copy-start.7
  51.3 0.8 copy-done.7
  52.1 0.0 copy-start.3
  52.1 15.0 %weights.1.unit = bf16[4,96,128]{2,1,0:T(8,128)(2,1)S(1)} custom-call(bf16[32,6,32,128]{3,2,1,0:T(8,128)(2,1)S(1)} %copy-done.2, bf16[8,16,128]{2,1,0:T(8,128)(2,1)S(1)} %copy-done.7, f32[64,64]{1,0:T(8,128)S(1)} %pad_maximum_fusion.steer), custom_call_target="tpu_custom_call" | custom-call | tf_op jit(solution)/shard_map/weights/pallas_call | solution.py:371
  67.0 0.0 copy-start.5
  67.0 0.6 copy-done.5
  67.7 15.9 %gather.1 = bf16[8,4,96,128]{3,2,1,0:T(8,128)(2,1)} custom-call(bf16[4,96,128]{2,1,0:T(8,128)(2,1)} %copy-done.5), custom_call_target="tpu_custom_call" | custom-call | tf_op jit(solution)/shard_map/gather/pallas_call | solution.py:380
  83.6 0.0 copy-done.3
  83.6 0.0 copy-start.1
  83.6 1.1 %copy-done.1 = bf16[8,4,96,128]{3,2,1,0:T(8,128)(2,1)S(1)} copy-done((bf16[8,4,96,128]{3,2,1,0:T(8,128)(2,1)S(1)}, bf16[8,4,96,128]{3,2,1,0:T(8,128)(2,1)}, u32[]{:S(2)}) %copy-start.1) | copy-done | bytes 786456
  84.8 5.3 %beams.1 = f32[32,128,256]{2,1,0:T(8,128)} custom-call(bf16[4,34,32,128]{3,2,1,0:T(8,128)(2,1)S(1)} %copy-done.3, bf16[32,96,128]{2,1,0:T(8,128)(2,1)S(1)} %bitcast.2), custom_call_target="tpu_custom_call" | custom-call | tf_op jit(solution)/shard_map/beams/pallas_call | solution.py:391
  (3 shorter events, 0.1 us)
Async XLA Ops:
  2.4 1.2 %copy-start.4 = (bf16[64,2,32,128]{3,2,1,0:T(8,128)(2,1)S(1)}, bf16[64,2,32,128]{3,2,1,0:T(8,128)(2,1)}, u32[]{:S(2)}) copy-start(bf16[64,2,32,128]{3,2,1,0:T(8,128)(2,1)} %echoes.1) | copy-start | bytes 3145732
  3.7 0.9 copy-start.6
  5.8 1.0 %copy-start = (bf16[136,32,128]{2,1,0:T(8,128)(2,1)}, bf16[136,32,128]{2,1,0:T(8,128)(2,1)S(1)}, u32[]{:S(2)}) copy-start(bf16[136,32,128]{2,1,0:T(8,128)(2,1)S(1)} %spectra.1.spec) | copy-start | bytes 3342340
  49.9 1.4 %copy-start.2 = (bf16[32,6,32,128]{3,2,1,0:T(8,128)(2,1)S(1)}, bf16[32,6,32,128]{3,2,1,0:T(8,128)(2,1)}, u32[]{:S(2)}) copy-start(bf16[32,6,32,128]{3,2,1,0:T(8,128)(2,1)} %get-tuple-element.9.mine) | copy-start | bytes 4718596
  51.3 0.8 copy-start.7
  52.1 31.6 %copy-start.3 = (bf16[4,34,32,128]{3,2,1,0:T(8,128)(2,1)S(1)}, bf16[4,34,32,128]{3,2,1,0:T(8,128)(2,1)}, u32[]{:S(2)}) copy-start(bf16[4,34,32,128]{3,2,1,0:T(8,128)(2,1)} %get-tuple-element.8.wide) | copy-start | bytes 3342340
  67.0 0.6 copy-start.5
  83.6 1.1 %copy-start.1 = (bf16[8,4,96,128]{3,2,1,0:T(8,128)(2,1)S(1)}, bf16[8,4,96,128]{3,2,1,0:T(8,128)(2,1)}, u32[]{:S(2)}) copy-start(bf16[8,4,96,128]{3,2,1,0:T(8,128)(2,1)} %gather.1) | copy-start | bytes 2359300

commit v3 on v2

--- a/solution.py
+++ b/solution.py
@@ -55,8 +55,8 @@
     return jnp.concatenate([jnp.cos(phases), jnp.sin(phases)], axis=0)
 
 
-def exchange_kernel(D, R, spec, mask, wide, mine, masks, send_m, recv_m, send_x, recv_x,
-                    send_w, recv_w, own):
+def exchange_kernel(D, R, spec, mask, mine, masks, send_m, recv_m, send_x, recv_x,
+                    own):
     N = D * R
     bins = PULSES // D
     share = bins // R
@@ -77,7 +77,6 @@
     local = [
         pltpu.make_async_copy(mask.at[g], masks.at[g], own.at[0]),
         pltpu.make_async_copy(spec.at[pl.ds(d * bins + g * share, share + 2)], mine.at[me], own.at[1]),
-        pltpu.make_async_copy(spec.at[pl.ds(d * bins, bins + 2)], wide.at[d], own.at[2]),
     ]
     for copy in local:
         copy.start()
@@ -94,12 +93,6 @@
         return pltpu.make_async_remote_copy(
             spec.at[pl.ds(td * bins + tg * share, share + 2)], mine.at[me], send_x.at[j],
             recv_x.at[me], device_id=(td, tg), device_id_type=MESH)
-
-    def wide_copy(j):
-        td = lax.rem(d + j, D)
-        return pltpu.make_async_remote_copy(
-            spec.at[pl.ds(td * bins, bins + 2)], wide.at[d], send_w.at[j], recv_w.at[d],
-            device_id=(td, g), device_id_type=MESH)
 
     def start(make):
         def run(j, c):
@@ -109,7 +102,6 @@
 
     lax.fori_loop(1, R, start(mask_copy), 0)
     lax.fori_loop(1, N, start(mine_copy), 0)
-    lax.fori_loop(1, D, start(wide_copy), 0)
 
     def end_mask(j, c):
         src = lax.rem(g + j, R)
@@ -127,6 +119,86 @@
             device_id=(sd, sg), device_id_type=MESH).wait_recv()
         return c
 
+    lax.fori_loop(1, R, end_mask, 0)
+    lax.fori_loop(1, N, end_mine, 0)
+    for copy in local:
+        copy.wait()
+
+
+def gather_kernel(D, R, share, unit, spec, out, wide, send, recv, cross_send, cross_recv, hand_send,
+                  hand_recv, send_w, recv_w, own):
+    H = R // 2
+    bins = PULSES // D
+    d, g = lax.axis_index("dop"), lax.axis_index("rng")
+    half = g // H * H
+    partner = lax.rem(g + H, R)
+    other = H - half
+    barrier = pltpu.get_barrier_semaphore()
+
+    def peer(j):
+        return half + lax.rem(g - half + j, H)
+
+    def greet(j, c):
+        pl.semaphore_signal(barrier, inc=1, device_id=(d, peer(j)), device_id_type=MESH)
+        return c
+
+    def greet_dop(j, c):
+        pl.semaphore_signal(barrier, inc=1, device_id=(lax.rem(d + j, D), g), device_id_type=MESH)
+        return c
+
+    lax.fori_loop(1, H, greet, 0)
+    lax.fori_loop(1, D, greet_dop, 0)
+    pl.semaphore_signal(barrier, inc=1, device_id=(d, partner), device_id_type=MESH)
+    local = [
+        pltpu.make_async_copy(unit, out.at[g], own.at[0]),
+        pltpu.make_async_copy(spec.at[pl.ds(d * bins, bins + 2)], wide.at[d], own.at[1]),
+    ]
+    for copy in local:
+        copy.start()
+    pl.semaphore_wait(barrier, H + D - 1)
+
+    def cross(b):
+        return pltpu.make_async_remote_copy(
+            unit.at[b], out.at[g, b], cross_send.at[b], cross_recv.at[b], device_id=(d, partner),
+            device_id_type=MESH)
+
+    def make(j):
+        return pltpu.make_async_remote_copy(
+            unit, out.at[g], send.at[j], recv.at[g], device_id=(d, peer(j)), device_id_type=MESH)
+
+    def hand(j, b):
+        return pltpu.make_async_remote_copy(
+            out.at[partner, b], out.at[partner, b], hand_send.at[j, b], hand_recv.at[partner, b],
+            device_id=(d, peer(j)), device_id_type=MESH)
+
+    def wide_copy(j):
+        td = lax.rem(d + j, D)
+        return pltpu.make_async_remote_copy(
+            spec.at[pl.ds(td * bins, bins + 2)], wide.at[d], send_w.at[j], recv_w.at[d],
+            device_id=(td, g), device_id_type=MESH)
+
+    def begin(j, c):
+        make(j).start()
+        return c
+
+    def begin_wide(j, c):
+        wide_copy(j).start()
+        return c
+
+    def end(j, c):
+        make(j).wait_send()
+        src = peer(j)
+        pltpu.make_async_remote_copy(
+            unit, out.at[src], send.at[j], recv.at[src], device_id=(d, src),
+            device_id_type=MESH).wait_recv()
+        far = other + lax.rem(g - half + j, H)
+        for b in range(share):
+            hand(j, b).wait_send()
+            pltpu.make_async_remote_copy(
+                unit.at[b], out.at[far, b], hand_send.at[j, b], hand_recv.at[far, b],
+                device_id=(d, src), device_id_type=MESH).wait_recv()
+        return c
+
     def end_wide(j, c):
         src = lax.rem(d + j, D)
         wide_copy(j).wait_send()
@@ -135,73 +207,26 @@
             device_id=(src, g), device_id_type=MESH).wait_recv()
         return c
 
-    lax.fori_loop(1, R, end_mask, 0)
-    lax.fori_loop(1, N, end_mine, 0)
+    for b in range(share):
+        cross(b).start()
+    lax.fori_loop(1, H, begin, 0)
+    lax.fori_loop(1, D, begin_wide, 0)
+    for b in range(share):
+        pltpu.make_async_remote_copy(
+            unit.at[b], out.at[partner, b], cross_send.at[b], cross_recv.at[b],
+            device_id=(d, partner), device_id_type=MESH).wait_recv()
+
+        def begin_hand(j, c):
+            hand(j, b).start()
+            return c
+
+        lax.fori_loop(1, H, begin_hand, 0)
+    lax.fori_loop(1, H, end, 0)
     lax.fori_loop(1, D, end_wide, 0)
+    for b in range(share):
+        cross(b).wait_send()
     for copy in local:
         copy.wait()
-
-
-def gather_kernel(R, unit, out, send, recv, pass_on, own):
-    H = R // 2
-    d, g = lax.axis_index("dop"), lax.axis_index("rng")
-    half = g // H * H
-    partner = lax.rem(g + H, R)
-    other = H - half
-    barrier = pltpu.get_barrier_semaphore()
-
-    def peer(j):
-        return half + lax.rem(g - half + j, H)
-
-    def greet(j, c):
-        pl.semaphore_signal(barrier, inc=1, device_id=(d, peer(j)), device_id_type=MESH)
-        return c
-
-    lax.fori_loop(1, H, greet, 0)
-    pl.semaphore_signal(barrier, inc=1, device_id=(d, partner), device_id_type=MESH)
-    local = pltpu.make_async_copy(unit, out.at[g], own)
-    local.start()
-    pl.semaphore_wait(barrier, H)
-
-    cross = pltpu.make_async_remote_copy(
-        unit, out.at[g], send.at[0], recv.at[g], device_id=(d, partner), device_id_type=MESH)
-    cross.start()
-
-    def make(j):
-        return pltpu.make_async_remote_copy(
-            unit, out.at[g], send.at[j], recv.at[g], device_id=(d, peer(j)), device_id_type=MESH)
-
-    def hand(j):
-        return pltpu.make_async_remote_copy(
-            out.at[partner], out.at[partner], pass_on.at[j], recv.at[partner],
-            device_id=(d, peer(j)), device_id_type=MESH)
-
-    def arrive(src):
-        pltpu.make_async_remote_copy(
-            unit, out.at[src], send.at[0], recv.at[src], device_id=(d, partner),
-            device_id_type=MESH).wait_recv()
-
-    def begin(j, c):
-        make(j).start()
-        return c
-
-    def begin_hand(j, c):
-        hand(j).start()
-        return c
-
-    def end(j, c):
-        make(j).wait_send()
-        hand(j).wait_send()
-        arrive(peer(j))
-        arrive(other + lax.rem(g - half + j, H))
-        return c
-
-    lax.fori_loop(1, H, begin, 0)
-    arrive(partner)
-    lax.fori_loop(1, H, begin_hand, 0)
-    lax.fori_loop(1, H, end, 0)
-    cross.wait_send()
-    local.wait()
 
 
 def invert(re, im):
@@ -355,16 +380,15 @@
         compiler_params=pltpu.CompilerParams(vmem_limit_bytes=32 * 1024 * 1024),
         name="spectra",
     )(echoes, twiddle_table(rows))
-    wide, mine, masks = pl.pallas_call(
+    mine, masks = pl.pallas_call(
         functools.partial(exchange_kernel, D, R),
         out_shape=[
-            jax.ShapeDtypeStruct((D, bins + 2, CH, 2 * cells), bf16),
             jax.ShapeDtypeStruct((N, share + 2, CH, 2 * cells), bf16),
             jax.ShapeDtypeStruct(mask.shape, bf16),
         ],
         in_specs=[anywhere] * 2,
-        out_specs=[anywhere] * 3,
-        scratch_shapes=[dma((R,)), dma((R,)), dma((N,)), dma((N,)), dma((D,)), dma((D,)), dma((3,))],
+        out_specs=[anywhere] * 2,
+        scratch_shapes=[dma((R,)), dma((R,)), dma((N,)), dma((N,)), dma((2,))],
         compiler_params=pltpu.CompilerParams(collective_id=0, has_side_effects=True),
         name="exchange",
     )(spec, mask)
@@ -377,15 +401,21 @@
         compiler_params=pltpu.CompilerParams(vmem_limit_bytes=32 * 1024 * 1024),
         name="weights",
     )(mine, masks, steer)
-    units = pl.pallas_call(
-        functools.partial(gather_kernel, R),
-        out_shape=jax.ShapeDtypeStruct((R,) + unit.shape, bf16),
-        in_specs=[anywhere],
-        out_specs=anywhere,
-        scratch_shapes=[dma((R,)), dma((R,)), dma((R,)), dma],
+    units, wide = pl.pallas_call(
+        functools.partial(gather_kernel, D, R, share),
+        out_shape=[
+            jax.ShapeDtypeStruct((R,) + unit.shape, bf16),
+            jax.ShapeDtypeStruct((D, bins + 2, CH, 2 * cells), bf16),
+        ],
+        in_specs=[anywhere] * 2,
+        out_specs=[anywhere] * 2,
+        scratch_shapes=[
+            dma((R,)), dma((R,)), dma((share,)), dma((share,)), dma((R, share)), dma((R, share)),
+            dma((D,)), dma((D,)), dma((2,)),
+        ],
         compiler_params=pltpu.CompilerParams(collective_id=1, has_side_effects=True),
         name="gather",
-    )(unit)
+    )(unit, spec)
     units = units.reshape(bins, 3 * CH, 2 * LOOKS)
     step_bins = 4
     out = pl.pallas_call(

time: 90.7 us -> 94.6 us (1.043)
  the two profiles are of different devices: /device:TPU:14 before, /device:TPU:1 now
where the time goes in v3:
time: 94.6 us; the launch traced here: 94.2 us
  Pallas kernels  83.4 us (88%)
  local copies, waits for them, and re-layouts  9.13 us (10%)
  other arithmetic  1.57 us (2%)
    pallas_call x1, Pallas kernels, body(): pl.pallas_call(functools.partial(exchange_kernel, D, R), out_shape=[jax.S...  34.2 us
    pallas_call x1, Pallas kernels, body(): pl.pallas_call(functools.partial(gather_kernel, D, R, share), out_shape=[...  27.6 us
    pallas_call x1, Pallas kernels, body(): pl.pallas_call(functools.partial(weights_kernel, D, R, share), out_shape=...  15 us
    unnamed x16, local copies, waits for them, and re-layouts  8.28 us
    pallas_call x1, Pallas kernels, body(): pl.pallas_call(functools.partial(beams_kernel, D, step_bins), grid=(bins...  5.33 us

profile of v3, /device:TPU:1, one launch (start us, length us, event | category | flops | bytes accessed | tf_op | source)
XLA Modules:
  0.0 94.2 jit_solution(14345940022923262852)
XLA Ops:
  0.0 0.7 multiply_add_fusion
  0.7 0.8 convert_element_type.13
  1.4 0.1 broadcast_in_dim.4
  1.5 0.1 multiply_cosine_fusion
  1.7 0.7 reshape.18.mask
  2.4 0.0 copy-start.3
  2.4 1.2 %copy-done.3 = bf16[64,2,32,128]{3,2,1,0:T(8,128)(2,1)S(1)} copy-done((bf16[64,2,32,128]{3,2,1,0:T(8,128)(2,1)S(1)}, bf16[64,2,32,128]{3,2,1,0:T(8,128)(2,1)}, u32[]{:S(2)}) %copy-start.3) | copy-done | bytes 1048600
  3.7 0.0 copy-start.6
  3.7 0.9 copy-done.6
  4.6 1.3 %spectra.1.spec = bf16[136,32,128]{2,1,0:T(8,128)(2,1)S(1)} custom-call(bf16[64,2,32,128]{3,2,1,0:T(8,128)(2,1)S(1)} %copy-done.3, bf16[136,256]{1,0:T(8,128)(2,1)S(1)} %copy-done.6), custom_call_target="tpu_custom_call" | custom-call | tf_op jit(solution)/shard_map/spectra/pallas_call | solution.py:375
  5.9 0.0 copy-start
  5.9 1.0 %copy-done = bf16[136,32,128]{2,1,0:T(8,128)(2,1)} copy-done((bf16[136,32,128]{2,1,0:T(8,128)(2,1)}, bf16[136,32,128]{2,1,0:T(8,128)(2,1)S(1)}, u32[]{:S(2)}) %copy-start) | copy-done | bytes 1114136
  6.8 34.2 %exchange.1 = (bf16[32,6,32,128]{3,2,1,0:T(8,128)(2,1)}, bf16[8,16,128]{2,1,0:T(8,128)(2,1)}) custom-call(bf16[136,32,128]{2,1,0:T(8,128)(2,1)} %copy-done, bf16[8,16,128]{2,1,0:T(8,128)(2,1)} %reshape.18.mask), custom_call_target="tpu_custom_call" | custom-call | tf_op jit(solution)/shard_map/exchange/pallas_call | solution.py:383
  41.1 0.0 copy-start.1
  41.1 1.4 %copy-done.1 = bf16[32,6,32,128]{3,2,1,0:T(8,128)(2,1)S(1)} copy-done((bf16[32,6,32,128]{3,2,1,0:T(8,128)(2,1)S(1)}, bf16[32,6,32,128]{3,2,1,0:T(8,128)(2,1)}, u32[]{:S(2)}) %copy-start.1) | copy-done | bytes 1572888
  42.5 0.0 copy-start.7
  42.5 0.8 copy-done.7
  43.3 15.0 %weights.1.unit = bf16[4,96,128]{2,1,0:T(8,128)(2,1)S(1)} custom-call(bf16[32,6,32,128]{3,2,1,0:T(8,128)(2,1)S(1)} %copy-done.1, bf16[8,16,128]{2,1,0:T(8,128)(2,1)S(1)} %copy-done.7, f32[64,64]{1,0:T(8,128)S(1)} %pad_maximum_fusion.steer), custom_call_target="tpu_custom_call" | custom-call | tf_op jit(solution)/shard_map/weights/pallas_call | solution.py:395
  58.2 0.0 copy-start.5
  58.2 0.7 copy-done.5
  58.9 27.6 %gather.1 = (bf16[8,4,96,128]{3,2,1,0:T(8,128)(2,1)}, bf16[4,34,32,128]{3,2,1,0:T(8,128)(2,1)}) custom-call(bf16[4,96,128]{2,1,0:T(8,128)(2,1)} %copy-done.5, bf16[136,32,128]{2,1,0:T(8,128)(2,1)} %copy-done), custom_call_target="tpu_custom_call" | custom-call | tf_op jit(solution)/shard_map/gather/pallas_call | solution.py:404
  86.5 0.0 copy-start.2
  86.5 1.2 %copy-done.2 = bf16[4,34,32,128]{3,2,1,0:T(8,128)(2,1)S(1)} copy-done((bf16[4,34,32,128]{3,2,1,0:T(8,128)(2,1)S(1)}, bf16[4,34,32,128]{3,2,1,0:T(8,128)(2,1)}, u32[]{:S(2)}) %copy-start.2) | copy-done | bytes 1114136
  87.7 0.0 copy-start.4
  87.7 1.1 %copy-done.4 = bf16[8,4,96,128]{3,2,1,0:T(8,128)(2,1)S(1)} copy-done((bf16[8,4,96,128]{3,2,1,0:T(8,128)(2,1)S(1)}, bf16[8,4,96,128]{3,2,1,0:T(8,128)(2,1)}, u32[]{:S(2)}) %copy-start.4) | copy-done | bytes 786456
  88.8 5.3 %beams.1 = f32[32,128,256]{2,1,0:T(8,128)} custom-call(bf16[4,34,32,128]{3,2,1,0:T(8,128)(2,1)S(1)} %copy-done.2, bf16[32,96,128]{2,1,0:T(8,128)(2,1)S(1)} %bitcast.2), custom_call_target="tpu_custom_call" | custom-call | tf_op jit(solution)/shard_map/beams/pallas_call | solution.py:421
  (3 shorter events, 0.1 us)
Async XLA Ops:
  2.4 1.2 %copy-start.3 = (bf16[64,2,32,128]{3,2,1,0:T(8,128)(2,1)S(1)}, bf16[64,2,32,128]{3,2,1,0:T(8,128)(2,1)}, u32[]{:S(2)}) copy-start(bf16[64,2,32,128]{3,2,1,0:T(8,128)(2,1)} %echoes.1) | copy-start | bytes 3145732
  3.7 0.9 copy-start.6
  5.9 1.0 %copy-start = (bf16[136,32,128]{2,1,0:T(8,128)(2,1)}, bf16[136,32,128]{2,1,0:T(8,128)(2,1)S(1)}, u32[]{:S(2)}) copy-start(bf16[136,32,128]{2,1,0:T(8,128)(2,1)S(1)} %spectra.1.spec) | copy-start | bytes 3342340
  41.1 1.4 %copy-start.1 = (bf16[32,6,32,128]{3,2,1,0:T(8,128)(2,1)S(1)}, bf16[32,6,32,128]{3,2,1,0:T(8,128)(2,1)}, u32[]{:S(2)}) copy-start(bf16[32,6,32,128]{3,2,1,0:T(8,128)(2,1)} %get-tuple-element.9.mine) | copy-start | bytes 4718596
  42.5 0.8 copy-start.7
  58.2 0.7 copy-start.5
  86.5 1.2 %copy-start.2 = (bf16[4,34,32,128]{3,2,1,0:T(8,128)(2,1)S(1)}, bf16[4,34,32,128]{3,2,1,0:T(8,128)(2,1)}, u32[]{:S(2)}) copy-start(bf16[4,34,32,128]{3,2,1,0:T(8,128)(2,1)} %get-tuple-element.11.wide) | copy-start | bytes 3342340
  87.7 1.1 %copy-start.4 = (bf16[8,4,96,128]{3,2,1,0:T(8,128)(2,1)S(1)}, bf16[8,4,96,128]{3,2,1,0:T(8,128)(2,1)}, u32[]{:S(2)}) copy-start(bf16[8,4,96,128]{3,2,1,0:T(8,128)(2,1)} %get-tuple-element.12) | copy-start | bytes 2359300

commit v4 on v2

--- a/solution.py
+++ b/solution.py
@@ -30,7 +30,17 @@
     return jnp.asarray(np.concatenate([np.cos(angles), np.sin(angles)], axis=1), bf16)
 
 
-def spectra_kernel(group, echoes, table, spec):
+def spectra_kernel(group, D, R, echoes, table, training, spec, mask):
+    cells = echoes.shape[0]
+    share = training.shape[0] // R
+    trains = training[...].astype(f32)
+    pieces = [trains[:, s * cells:(s + 1) * cells] for s in range(D)]
+    pieces = [jnp.concatenate([piece, piece], axis=1) for piece in pieces]
+    spare = jnp.zeros((-share * D % 16, 2 * cells), f32)
+    for g in range(R):
+        lines = [piece[g * share:(g + 1) * share] for piece in pieces]
+        lines = lines + [spare] if spare.shape[0] else lines
+        mask[g] = jnp.concatenate(lines, axis=0).astype(bf16)
     left = table[...]
     for first in range(0, CH, group):
         real, imag = [
@@ -142,7 +152,8 @@
         copy.wait()
 
 
-def gather_kernel(R, unit, out, send, recv, pass_on, own):
+def gather_kernel(R, share, unit, out, send, recv, cross_send, cross_recv, hand_send,
+                  hand_recv, own):
     H = R // 2
     d, g = lax.axis_index("dop"), lax.axis_index("rng")
     half = g // H * H
@@ -159,49 +170,63 @@
 
     lax.fori_loop(1, H, greet, 0)
     pl.semaphore_signal(barrier, inc=1, device_id=(d, partner), device_id_type=MESH)
-    local = pltpu.make_async_copy(unit, out.at[g], own)
-    local.start()
+    local = [
+        pltpu.make_async_copy(unit, out.at[g], own),
+    ]
+    for copy in local:
+        copy.start()
     pl.semaphore_wait(barrier, H)
 
-    cross = pltpu.make_async_remote_copy(
-        unit, out.at[g], send.at[0], recv.at[g], device_id=(d, partner), device_id_type=MESH)
-    cross.start()
+    def cross(b):
+        return pltpu.make_async_remote_copy(
+            unit.at[b], out.at[g, b], cross_send.at[b], cross_recv.at[b], device_id=(d, partner),
+            device_id_type=MESH)
 
     def make(j):
         return pltpu.make_async_remote_copy(
             unit, out.at[g], send.at[j], recv.at[g], device_id=(d, peer(j)), device_id_type=MESH)
 
-    def hand(j):
-        return pltpu.make_async_remote_copy(
-            out.at[partner], out.at[partner], pass_on.at[j], recv.at[partner],
+    def hand(j, b):
+        return pltpu.make_async_remote_copy(
+            out.at[partner, b], out.at[partner, b], hand_send.at[j, b], hand_recv.at[partner, b],
             device_id=(d, peer(j)), device_id_type=MESH)
-
-    def arrive(src):
-        pltpu.make_async_remote_copy(
-            unit, out.at[src], send.at[0], recv.at[src], device_id=(d, partner),
-            device_id_type=MESH).wait_recv()
 
     def begin(j, c):
         make(j).start()
         return c
 
-    def begin_hand(j, c):
-        hand(j).start()
-        return c
-
     def end(j, c):
         make(j).wait_send()
-        hand(j).wait_send()
-        arrive(peer(j))
-        arrive(other + lax.rem(g - half + j, H))
-        return c
-
+        src = peer(j)
+        pltpu.make_async_remote_copy(
+            unit, out.at[src], send.at[j], recv.at[src], device_id=(d, src),
+            device_id_type=MESH).wait_recv()
+        far = other + lax.rem(g - half + j, H)
+        for b in range(share):
+            hand(j, b).wait_send()
+            pltpu.make_async_remote_copy(
+                unit.at[b], out.at[far, b], hand_send.at[j, b], hand_recv.at[far, b],
+                device_id=(d, src), device_id_type=MESH).wait_recv()
+        return c
+
+    for b in range(share):
+        cross(b).start()
     lax.fori_loop(1, H, begin, 0)
-    arrive(partner)
-    lax.fori_loop(1, H, begin_hand, 0)
+    for b in range(share):
+        pltpu.make_async_remote_copy(
+            unit.at[b], out.at[partner, b], cross_send.at[b], cross_recv.at[b],
+            device_id=(d, partner), device_id_type=MESH).wait_recv()
+
+        def begin_hand(j, c):
+            hand(j, b).start()
+            return c
+
+        lax.fori_loop(1, H, begin_hand, 0)
     lax.fori_loop(1, H, end, 0)
-    cross.wait_send()
-    local.wait()
+    for b in range(share):
+        cross(b).wait_send()
+    for copy in local:
+        copy.wait()
 
 
 def invert(re, im):
@@ -265,7 +290,7 @@
         turned_k = [jnp.concatenate(line, axis=1) for line in turned]
         for b in range(share):
             weight = jnp.concatenate(
-                [jnp.broadcast_to(rows[b * D + s:b * D + s + 1], (CH, 128)).astype(bf16)
+                [jnp.broadcast_to(rows[s * share + b:s * share + b + 1], (CH, 128)).astype(bf16)
                  for s in range(D)], axis=1)
             left = jnp.concatenate([plain_k[b + i] * weight for i in range(3)], axis=0)
             right = jnp.concatenate(
@@ -340,21 +365,21 @@
     share = bins // R
     cells = echoes.shape[0]
     rows = PULSES + 8
-    mask = training.astype(bf16).reshape(R, share, D, 1, cells)
-    mask = jnp.broadcast_to(mask, (R, share, D, 2, cells)).reshape(R, share * D, 2 * cells)
-    mask = jnp.pad(mask, ((0, 0), (0, -share * D % 16), (0, 0)))
     steer = steering(look_index)
     anywhere = pl.BlockSpec(memory_space=pl.ANY)
     in_vmem = pl.BlockSpec(memory_space=pltpu.VMEM)
     dma = pltpu.SemaphoreType.DMA
-    spec = pl.pallas_call(
-        functools.partial(spectra_kernel, 16),
-        out_shape=jax.ShapeDtypeStruct((rows, CH, 2 * cells), bf16),
-        in_specs=[in_vmem] * 2,
-        out_specs=in_vmem,
+    spec, mask = pl.pallas_call(
+        functools.partial(spectra_kernel, 16, D, R),
+        out_shape=[
+            jax.ShapeDtypeStruct((rows, CH, 2 * cells), bf16),
+            jax.ShapeDtypeStruct((R, share * D + -share * D % 16, 2 * cells), bf16),
+        ],
+        in_specs=[in_vmem] * 3,
+        out_specs=[in_vmem] * 2,
         compiler_params=pltpu.CompilerParams(vmem_limit_bytes=32 * 1024 * 1024),
         name="spectra",
-    )(echoes, twiddle_table(rows))
+    )(echoes, twiddle_table(rows), training)
     wide, mine, masks = pl.pallas_call(
         functools.partial(exchange_kernel, D, R),
         out_shape=[
@@ -378,11 +403,13 @@
         name="weights",
     )(mine, masks, steer)
     units = pl.pallas_call(
-        functools.partial(gather_kernel, R),
+        functools.partial(gather_kernel, R, share),
         out_shape=jax.ShapeDtypeStruct((R,) + unit.shape, bf16),
         in_specs=[anywhere],
         out_specs=anywhere,
-        scratch_shapes=[dma((R,)), dma((R,)), dma((R,)), dma],
+        scratch_shapes=[
+            dma((R,)), dma((R,)), dma((share,)), dma((share,)), dma((R, share)), dma((R, share)), dma,
+        ],
         compiler_params=pltpu.CompilerParams(collective_id=1, has_side_effects=True),
         name="gather",
     )(unit)

time: 90.7 us -> 91 us (level)
    unnamed x16 -> x20, local copies, waits for them, and re-layouts: 7.03 us -> 8.39 us
where the time goes in v4:
time: 91 us; the launch traced here: 89.8 us
  Pallas kernels  80.5 us (88%)
  local copies, waits for them, and re-layouts  8.39 us (9%)
    pallas_call x1, Pallas kernels, body(): pl.pallas_call(functools.partial(exchange_kernel, D, R), out_shape=[jax.S...  43 us
    pallas_call x1, Pallas kernels, body(): pl.pallas_call(functools.partial(gather_kernel, R, share), out_shape=jax....  15.9 us
    pallas_call x1, Pallas kernels, body(): pl.pallas_call(functools.partial(weights_kernel, D, R, share), out_shape=...  15 us
    unnamed x20, local copies, waits for them, and re-layouts  8.39 us
    pallas_call x1, Pallas kernels, body(): pl.pallas_call(functools.partial(beams_kernel, D, step_bins), grid=(bins...  5.33 us

profile of v4, /device:TPU:14, one launch (start us, length us, event | category | flops | bytes accessed | tf_op | source)
XLA Modules:
  0.0 89.8 jit_solution(7773201749843071542)
XLA Ops:
  0.0 0.7 multiply_add_fusion
  0.7 0.1 multiply_cosine_fusion
  0.8 0.0 copy-start.4
  0.8 1.2 %copy-done.4 = bf16[64,2,32,128]{3,2,1,0:T(8,128)(2,1)S(1)} copy-done((bf16[64,2,32,128]{3,2,1,0:T(8,128)(2,1)S(1)}, bf16[64,2,32,128]{3,2,1,0:T(8,128)(2,1)}, u32[]{:S(2)}) %copy-start.4) | copy-done | bytes 1048600
  2.1 0.0 copy-start.6
  2.1 0.9 copy-done.6
  2.9 0.0 copy-start.7
  2.9 0.8 copy-done.7
  3.7 1.3 %spectra.1 = (bf16[136,32,128]{2,1,0:T(8,128)(2,1)S(1)}, bf16[8,16,128]{2,1,0:T(8,128)(2,1)S(1)}) custom-call(bf16[64,2,32,128]{3,2,1,0:T(8,128)(2,1)S(1)} %copy-done.4, bf16[136,256]{1,0:T(8,128)(2,1)S(1)} %copy-done.6, s32[32,256]{1,0:T(8,128)S(1)} %copy-done.7), custom_call_target="tpu_custom_call" | custom-call | tf_op jit(solution)/shard_map/spectra/pallas_call | solution.py:372
  5.0 0.0 copy-start.3
  5.0 1.0 %copy-done.3 = bf16[136,32,128]{2,1,0:T(8,128)(2,1)} copy-done((bf16[136,32,128]{2,1,0:T(8,128)(2,1)}, bf16[136,32,128]{2,1,0:T(8,128)(2,1)S(1)}, u32[]{:S(2)}) %copy-start.3) | copy-done | bytes 1114136
  6.0 0.0 copy-start.8
  6.0 0.6 copy-done.8
  6.6 43.0 %exchange.1 = (bf16[4,34,32,128]{3,2,1,0:T(8,128)(2,1)}, bf16[32,6,32,128]{3,2,1,0:T(8,128)(2,1)}, bf16[8,16,128]{2,1,0:T(8,128)(2,1)}) custom-call(bf16[136,32,128]{2,1,0:T(8,128)(2,1)} %copy-done.3, bf16[8,16,128]{2,1,0:T(8,128)(2,1)} %copy-done.8), custom_call_target="tpu_custom_call" | custom-call | tf_op jit(solution)/shard_map/exchange/pallas_call | solution.py:383
  49.7 0.0 copy-start.1
  49.7 1.4 %copy-done.1 = bf16[32,6,32,128]{3,2,1,0:T(8,128)(2,1)S(1)} copy-done((bf16[32,6,32,128]{3,2,1,0:T(8,128)(2,1)S(1)}, bf16[32,6,32,128]{3,2,1,0:T(8,128)(2,1)}, u32[]{:S(2)}) %copy-start.1) | copy-done | bytes 1572888
  51.1 0.0 copy-start.9
  51.1 0.8 copy-done.9
  51.8 0.0 copy-start.2
  51.8 15.0 %weights.1.unit = bf16[4,96,128]{2,1,0:T(8,128)(2,1)S(1)} custom-call(bf16[32,6,32,128]{3,2,1,0:T(8,128)(2,1)S(1)} %copy-done.1, bf16[8,16,128]{2,1,0:T(8,128)(2,1)S(1)} %copy-done.9, f32[64,64]{1,0:T(8,128)S(1)} %pad_maximum_fusion.steer), custom_call_target="tpu_custom_call" | custom-call | tf_op jit(solution)/shard_map/weights/pallas_call | solution.py:396
  66.8 0.0 copy-start.5
  66.8 0.6 copy-done.5
  67.4 15.9 %gather.1 = bf16[8,4,96,128]{3,2,1,0:T(8,128)(2,1)} custom-call(bf16[4,96,128]{2,1,0:T(8,128)(2,1)} %copy-done.5), custom_call_target="tpu_custom_call" | custom-call | tf_op jit(solution)/shard_map/gather/pallas_call | solution.py:405
  83.3 0.0 copy-done.2
  83.3 0.0 copy-start
  83.3 1.1 %copy-done = bf16[8,4,96,128]{3,2,1,0:T(8,128)(2,1)S(1)} copy-done((bf16[8,4,96,128]{3,2,1,0:T(8,128)(2,1)S(1)}, bf16[8,4,96,128]{3,2,1,0:T(8,128)(2,1)}, u32[]{:S(2)}) %copy-start) | copy-done | bytes 786456
  84.5 5.3 %beams.1 = f32[32,128,256]{2,1,0:T(8,128)} custom-call(bf16[4,34,32,128]{3,2,1,0:T(8,128)(2,1)S(1)} %copy-done.2, bf16[32,96,128]{2,1,0:T(8,128)(2,1)S(1)} %bitcast.2), custom_call_target="tpu_custom_call" | custom-call | tf_op jit(solution)/shard_map/beams/pallas_call | solution.py:418
  (2 shorter events, 0.0 us)
Async XLA Ops:
  0.8 1.2 %copy-start.4 = (bf16[64,2,32,128]{3,2,1,0:T(8,128)(2,1)S(1)}, bf16[64,2,32,128]{3,2,1,0:T(8,128)(2,1)}, u32[]{:S(2)}) copy-start(bf16[64,2,32,128]{3,2,1,0:T(8,128)(2,1)} %echoes.1) | copy-start | bytes 3145732
  2.1 0.9 copy-start.6
  2.9 0.8 copy-start.7
  5.0 1.0 %copy-start.3 = (bf16[136,32,128]{2,1,0:T(8,128)(2,1)}, bf16[136,32,128]{2,1,0:T(8,128)(2,1)S(1)}, u32[]{:S(2)}) copy-start(bf16[136,32,128]{2,1,0:T(8,128)(2,1)S(1)} %get-tuple-element.10.spec) | copy-start | bytes 3342340
  6.0 0.6 copy-start.8
  49.7 1.4 %copy-start.1 = (bf16[32,6,32,128]{3,2,1,0:T(8,128)(2,1)S(1)}, bf16[32,6,32,128]{3,2,1,0:T(8,128)(2,1)}, u32[]{:S(2)}) copy-start(bf16[32,6,32,128]{3,2,1,0:T(8,128)(2,1)} %get-tuple-element.13.mine) | copy-start | bytes 4718596
  51.1 0.8 copy-start.9
  51.8 31.5 %copy-start.2 = (bf16[4,34,32,128]{3,2,1,0:T(8,128)(2,1)S(1)}, bf16[4,34,32,128]{3,2,1,0:T(8,128)(2,1)}, u32[]{:S(2)}) copy-start(bf16[4,34,32,128]{3,2,1,0:T(8,128)(2,1)} %get-tuple-element.12.wide) | copy-start | bytes 3342340
  66.8 0.6 copy-start.5
  83.3 1.1 %copy-start = (bf16[8,4,96,128]{3,2,1,0:T(8,128)(2,1)S(1)}, bf16[8,4,96,128]{3,2,1,0:T(8,128)(2,1)}, u32[]{:S(2)}) copy-start(bf16[8,4,96,128]{3,2,1,0:T(8,128)(2,1)} %gather.1) | copy-start | bytes 2359300

commit v5 on v2

--- a/solution.py
+++ b/solution.py
@@ -30,7 +30,17 @@
     return jnp.asarray(np.concatenate([np.cos(angles), np.sin(angles)], axis=1), bf16)
 
 
-def spectra_kernel(group, echoes, table, spec):
+def spectra_kernel(group, D, R, echoes, table, training, spec, mask):
+    cells = echoes.shape[0]
+    share = training.shape[0] // R
+    trains = training[...].astype(f32)
+    pieces = [trains[:, s * cells:(s + 1) * cells] for s in range(D)]
+    pieces = [jnp.concatenate([piece, piece], axis=1) for piece in pieces]
+    spare = jnp.zeros((-share * D % 16, 2 * cells), f32)
+    for g in range(R):
+        lines = [piece[g * share:(g + 1) * share] for piece in pieces]
+        lines = lines + [spare] if spare.shape[0] else lines
+        mask[g] = jnp.concatenate(lines, axis=0).astype(bf16)
     left = table[...]
     for first in range(0, CH, group):
         real, imag = [
@@ -265,7 +275,7 @@
         turned_k = [jnp.concatenate(line, axis=1) for line in turned]
         for b in range(share):
             weight = jnp.concatenate(
-                [jnp.broadcast_to(rows[b * D + s:b * D + s + 1], (CH, 128)).astype(bf16)
+                [jnp.broadcast_to(rows[s * share + b:s * share + b + 1], (CH, 128)).astype(bf16)
                  for s in range(D)], axis=1)
             left = jnp.concatenate([plain_k[b + i] * weight for i in range(3)], axis=0)
             right = jnp.concatenate(
@@ -340,21 +350,21 @@
     share = bins // R
     cells = echoes.shape[0]
     rows = PULSES + 8
-    mask = training.astype(bf16).reshape(R, share, D, 1, cells)
-    mask = jnp.broadcast_to(mask, (R, share, D, 2, cells)).reshape(R, share * D, 2 * cells)
-    mask = jnp.pad(mask, ((0, 0), (0, -share * D % 16), (0, 0)))
     steer = steering(look_index)
     anywhere = pl.BlockSpec(memory_space=pl.ANY)
     in_vmem = pl.BlockSpec(memory_space=pltpu.VMEM)
     dma = pltpu.SemaphoreType.DMA
-    spec = pl.pallas_call(
-        functools.partial(spectra_kernel, 16),
-        out_shape=jax.ShapeDtypeStruct((rows, CH, 2 * cells), bf16),
-        in_specs=[in_vmem] * 2,
-        out_specs=in_vmem,
+    spec, mask = pl.pallas_call(
+        functools.partial(spectra_kernel, 16, D, R),
+        out_shape=[
+            jax.ShapeDtypeStruct((rows, CH, 2 * cells), bf16),
+            jax.ShapeDtypeStruct((R, share * D + -share * D % 16, 2 * cells), bf16),
+        ],
+        in_specs=[in_vmem] * 3,
+        out_specs=[in_vmem] * 2,
         compiler_params=pltpu.CompilerParams(vmem_limit_bytes=32 * 1024 * 1024),
         name="spectra",
-    )(echoes, twiddle_table(rows))
+    )(echoes, twiddle_table(rows), training)
     wide, mine, masks = pl.pallas_call(
         functools.partial(exchange_kernel, D, R),
         out_shape=[

time: 90.7 us -> 90.5 us (level)
    unnamed x16 -> x20, local copies, waits for them, and re-layouts: 7.03 us -> 8.39 us
where the time goes in v5:
time: 90.5 us; the launch traced here: 89.8 us
  Pallas kernels  80.5 us (89%)
  local copies, waits for them, and re-layouts  8.39 us (9%)
    pallas_call x1, Pallas kernels, body(): pl.pallas_call(functools.partial(exchange_kernel, D, R), out_shape=[jax.S...  43 us
    pallas_call x1, Pallas kernels, body(): pl.pallas_call(functools.partial(gather_kernel, R), out_shape=jax.ShapeDt...  15.9 us
    pallas_call x1, Pallas kernels, body(): pl.pallas_call(functools.partial(weights_kernel, D, R, share), out_shape=...  15 us
    unnamed x20, local copies, waits for them, and re-layouts  8.39 us
    pallas_call x1, Pallas kernels, body(): pl.pallas_call(functools.partial(beams_kernel, D, step_bins), grid=(bins...  5.33 us

profile of v5, /device:TPU:14, one launch (start us, length us, event | category | flops | bytes accessed | tf_op | source)
XLA Modules:
  0.0 89.8 jit_solution(7365382268861619325)
XLA Ops:
  0.0 0.7 multiply_add_fusion
  0.7 0.1 multiply_cosine_fusion
  0.8 0.0 copy-start.4
  0.8 1.2 %copy-done.4 = bf16[64,2,32,128]{3,2,1,0:T(8,128)(2,1)S(1)} copy-done((bf16[64,2,32,128]{3,2,1,0:T(8,128)(2,1)S(1)}, bf16[64,2,32,128]{3,2,1,0:T(8,128)(2,1)}, u32[]{:S(2)}) %copy-start.4) | copy-done | bytes 1048600
  2.1 0.0 copy-start.6
  2.1 0.9 copy-done.6
  2.9 0.0 copy-start.7
  2.9 0.8 copy-done.7
  3.7 1.3 %spectra.1 = (bf16[136,32,128]{2,1,0:T(8,128)(2,1)S(1)}, bf16[8,16,128]{2,1,0:T(8,128)(2,1)S(1)}) custom-call(bf16[64,2,32,128]{3,2,1,0:T(8,128)(2,1)S(1)} %copy-done.4, bf16[136,256]{1,0:T(8,128)(2,1)S(1)} %copy-done.6, s32[32,256]{1,0:T(8,128)S(1)} %copy-done.7), custom_call_target="tpu_custom_call" | custom-call | tf_op jit(solution)/shard_map/spectra/pallas_call | solution.py:357
  5.0 0.0 copy-start.3
  5.0 1.0 %copy-done.3 = bf16[136,32,128]{2,1,0:T(8,128)(2,1)} copy-done((bf16[136,32,128]{2,1,0:T(8,128)(2,1)}, bf16[136,32,128]{2,1,0:T(8,128)(2,1)S(1)}, u32[]{:S(2)}) %copy-start.3) | copy-done | bytes 1114136
  6.0 0.0 copy-start.8
  6.0 0.6 copy-done.8
  6.6 43.0 %exchange.1 = (bf16[4,34,32,128]{3,2,1,0:T(8,128)(2,1)}, bf16[32,6,32,128]{3,2,1,0:T(8,128)(2,1)}, bf16[8,16,128]{2,1,0:T(8,128)(2,1)}) custom-call(bf16[136,32,128]{2,1,0:T(8,128)(2,1)} %copy-done.3, bf16[8,16,128]{2,1,0:T(8,128)(2,1)} %copy-done.8), custom_call_target="tpu_custom_call" | custom-call | tf_op jit(solution)/shard_map/exchange/pallas_call | solution.py:368
  49.7 0.0 copy-start.1
  49.7 1.4 %copy-done.1 = bf16[32,6,32,128]{3,2,1,0:T(8,128)(2,1)S(1)} copy-done((bf16[32,6,32,128]{3,2,1,0:T(8,128)(2,1)S(1)}, bf16[32,6,32,128]{3,2,1,0:T(8,128)(2,1)}, u32[]{:S(2)}) %copy-start.1) | copy-done | bytes 1572888
  51.1 0.0 copy-start.9
  51.1 0.8 copy-done.9
  51.8 0.0 copy-start.2
  51.8 15.0 %weights.1.unit = bf16[4,96,128]{2,1,0:T(8,128)(2,1)S(1)} custom-call(bf16[32,6,32,128]{3,2,1,0:T(8,128)(2,1)S(1)} %copy-done.1, bf16[8,16,128]{2,1,0:T(8,128)(2,1)S(1)} %copy-done.9, f32[64,64]{1,0:T(8,128)S(1)} %pad_maximum_fusion.steer), custom_call_target="tpu_custom_call" | custom-call | tf_op jit(solution)/shard_map/weights/pallas_call | solution.py:381
  66.8 0.0 copy-start.5
  66.8 0.6 copy-done.5
  67.4 15.9 %gather.1 = bf16[8,4,96,128]{3,2,1,0:T(8,128)(2,1)} custom-call(bf16[4,96,128]{2,1,0:T(8,128)(2,1)} %copy-done.5), custom_call_target="tpu_custom_call" | custom-call | tf_op jit(solution)/shard_map/gather/pallas_call | solution.py:390
  83.4 0.0 copy-done.2
  83.4 0.0 copy-start
  83.4 1.1 %copy-done = bf16[8,4,96,128]{3,2,1,0:T(8,128)(2,1)S(1)} copy-done((bf16[8,4,96,128]{3,2,1,0:T(8,128)(2,1)S(1)}, bf16[8,4,96,128]{3,2,1,0:T(8,128)(2,1)}, u32[]{:S(2)}) %copy-start) | copy-done | bytes 786456
  84.5 5.3 %beams.1 = f32[32,128,256]{2,1,0:T(8,128)} custom-call(bf16[4,34,32,128]{3,2,1,0:T(8,128)(2,1)S(1)} %copy-done.2, bf16[32,96,128]{2,1,0:T(8,128)(2,1)S(1)} %bitcast.2), custom_call_target="tpu_custom_call" | custom-call | tf_op jit(solution)/shard_map/beams/pallas_call | solution.py:401
  (2 shorter events, 0.0 us)
Async XLA Ops:
  0.8 1.2 %copy-start.4 = (bf16[64,2,32,128]{3,2,1,0:T(8,128)(2,1)S(1)}, bf16[64,2,32,128]{3,2,1,0:T(8,128)(2,1)}, u32[]{:S(2)}) copy-start(bf16[64,2,32,128]{3,2,1,0:T(8,128)(2,1)} %echoes.1) | copy-start | bytes 3145732
  2.1 0.9 copy-start.6
  2.9 0.8 copy-start.7
  5.0 1.0 %copy-start.3 = (bf16[136,32,128]{2,1,0:T(8,128)(2,1)}, bf16[136,32,128]{2,1,0:T(8,128)(2,1)S(1)}, u32[]{:S(2)}) copy-start(bf16[136,32,128]{2,1,0:T(8,128)(2,1)S(1)} %get-tuple-element.10.spec) | copy-start | bytes 3342340
  6.0 0.6 copy-start.8
  49.7 1.4 %copy-start.1 = (bf16[32,6,32,128]{3,2,1,0:T(8,128)(2,1)S(1)}, bf16[32,6,32,128]{3,2,1,0:T(8,128)(2,1)}, u32[]{:S(2)}) copy-start(bf16[32,6,32,128]{3,2,1,0:T(8,128)(2,1)} %get-tuple-element.13.mine) | copy-start | bytes 4718596
  51.1 0.8 copy-start.9
  51.8 31.5 %copy-start.2 = (bf16[4,34,32,128]{3,2,1,0:T(8,128)(2,1)S(1)}, bf16[4,34,32,128]{3,2,1,0:T(8,128)(2,1)}, u32[]{:S(2)}) copy-start(bf16[4,34,32,128]{3,2,1,0:T(8,128)(2,1)} %get-tuple-element.12.wide) | copy-start | bytes 3342340
  66.8 0.6 copy-start.5
  83.4 1.1 %copy-start = (bf16[8,4,96,128]{3,2,1,0:T(8,128)(2,1)S(1)}, bf16[8,4,96,128]{3,2,1,0:T(8,128)(2,1)}, u32[]{:S(2)}) copy-start(bf16[8,4,96,128]{3,2,1,0:T(8,128)(2,1)} %gather.1) | copy-start | bytes 2359300
